TPU v7x, 512 devices: a whole 4x4x16 slice. The times are simulated.
512 devices in a mesh: gx: 16 (over z), gy: 16 (over y, x), gz: 2 (over core).
Axes of the slice: x: 4, y: 4, z: 16, core: 2. Of those that a mesh axis runs over, the one named last changes fastest.
Arguments:
- source: float32 [128, 512, 256], P('gx', 'gy', 'gz'), may hold values from -8 to 8, as said below
- beta_cells: float32 [128, 512, 256], P('gx', 'gy', 'gz'), may hold values from 0.25 to 4
- target: int32 [16, 16, 2], P('gx', 'gy', 'gz'), may hold values from 0 to 15
Outputs:
- solution: float32 [128, 512, 256], P('gx', 'gy', 'gz')
Inputs may be any that keep to these rules, and one draw needn't show every extreme that they name: source is a real field of order one.
All inputs are finite; a program needn't handle non-finite values.
Results may differ from a plain program's by a relative error of at most 0.0001.
Values sent between devices are 32-bit elements; how exact they have to be, the bound alone decides.
A program may use at most 64 MiB of HBM per device.

v0:
```python
import jax
import jax.numpy as jnp
from jax import lax
from jax.sharding import PartitionSpec as P

BOTTOM = 6


WEIGHT = 0.8


def padded(shard, sides, width):
    for axis, dim in sides:
        peers, length = (lax.axis_size(axis), shard.shape[dim])
        up = [(i, (i + 1) % peers) for i in range(peers - 1)]
        down = [(j, i) for i, j in up]
        last = lax.slice_in_dim(shard, length - width, length, axis=dim)
        first = lax.slice_in_dim(shard, 0, width, axis=dim)
        before = lax.ppermute(last, axis, up)
        after = lax.ppermute(first, axis, down)
        shard = jnp.concatenate([before, shard, after], axis=dim)
    return shard


def pad_cells(field):
    widths = [(0, 0)] * (field.ndim - 3) + [(1, 1)] * 3
    return jnp.pad(field, widths)


def face_terms(padded_val, padded_coef):
    center_val = padded_val[..., 1:-1, 1:-1, 1:-1]
    center_coef = padded_coef[..., 1:-1, 1:-1, 1:-1]
    neighbours = [
        (padded_val[..., :-2, 1:-1, 1:-1], padded_coef[..., :-2, 1:-1, 1:-1]),
        (padded_val[..., 2:, 1:-1, 1:-1], padded_coef[..., 2:, 1:-1, 1:-1]),
        (padded_val[..., 1:-1, :-2, 1:-1], padded_coef[..., 1:-1, :-2, 1:-1]),
        (padded_val[..., 1:-1, 2:, 1:-1], padded_coef[..., 1:-1, 2:, 1:-1]),
        (padded_val[..., 1:-1, 1:-1, :-2], padded_coef[..., 1:-1, 1:-1, :-2]),
        (padded_val[..., 1:-1, 1:-1, 2:], padded_coef[..., 1:-1, 1:-1, 2:]),
    ]
    weight_sum = jnp.zeros_like(center_coef)
    flux_sum = jnp.zeros_like(center_val)
    for near_val, near_coef in neighbours:
        face_value = 0.5 * (center_coef + near_coef)
        weight_sum = weight_sum + face_value
        flux_sum = flux_sum + face_value * (center_val - near_val)
    return (center_val, weight_sum, flux_sum)


def relax_cells(padded_val, padded_coef, rhs_field, factor, spare_term):
    center_val, weight_sum, flux_sum = face_terms(padded_val, padded_coef)
    return center_val + WEIGHT * (rhs_field - factor * flux_sum) / (
        factor * weight_sum + spare_term
    )


def residual(padded_val, padded_coef, rhs_field, factor):
    center_val, weight_sum, flux_sum = face_terms(padded_val, padded_coef)
    return rhs_field - factor * flux_sum


def restrict(field):
    size_a, size_b, size_c = field.shape
    return field.reshape(size_a // 2, 2, size_b // 2, 2, size_c // 2, 2).mean(axis=(1, 3, 5))


def prolong(field):
    size_a, size_b, size_c = field.shape
    spread = jnp.broadcast_to(field[:, None, :, None, :, None], (size_a, 2, size_b, 2, size_c, 2))
    return spread.reshape(2 * size_a, 2 * size_b, 2 * size_c)


def bottom_solve(rhs_field, coefficient, inside):
    spare_term = 1.0 - inside
    padded_coef = pad_cells(coefficient)
    total = jnp.sum(rhs_field, axis=(-3, -2, -1), keepdims=True)
    count = jnp.sum(inside, axis=(-3, -2, -1), keepdims=True)
    mean_src = total / jnp.maximum(count, 1.0)
    approx = inside * (4.0 * mean_src)
    for number in range(BOTTOM):
        approx = inside * relax_cells(pad_cells(approx), padded_coef, rhs_field, 0.0625, spare_term)
    return approx


def fine_halo(field):
    return padded(field, (("gx", 0), ("gy", 1), ("gz", 2)), 1)


def post_halo(field):
    return padded(field, (("gx", 0), ("gy", 1), ("gz", 2)), 1)


def coarse_halo(field):
    return padded(field, (("gx", 0), ("gy", 1), ("gz", 2)), 1)


def per_device(source, beta_cells, target):
    fine_pad = fine_halo(beta_cells)
    fine_sol = relax_cells(pad_cells(jnp.zeros_like(source)), fine_pad, source, 1.0, 0.0)
    fine_sol = relax_cells(fine_halo(fine_sol), fine_pad, source, 1.0, 0.0)
    fine_res = residual(fine_halo(fine_sol), fine_pad, source, 1.0)
    mid_src = restrict(fine_res)
    mid_coef = restrict(beta_cells)
    mid_pad = coarse_halo(mid_coef)
    mid_sol = relax_cells(pad_cells(jnp.zeros_like(mid_src)), mid_pad, mid_src, 0.25, 0.0)
    mid_sol = relax_cells(coarse_halo(mid_sol), mid_pad, mid_src, 0.25, 0.0)
    mid_res = residual(coarse_halo(mid_sol), mid_pad, mid_src, 0.25)
    low_src = restrict(mid_res)
    low_coef = restrict(mid_coef)
    cells_x = low_src.shape[0]
    own_target = target[0, 0, 0]
    row_fields, row_targets = (
        lax.all_gather(jnp.stack([low_src, low_coef]), "gx", axis=1, tiled=True),
        lax.all_gather(target.astype(jnp.float32), "gx", axis=0, tiled=True),
    )
    owner_cells = jnp.repeat(row_targets[:, 0, 0], cells_x)
    inside = jnp.broadcast_to(
        (owner_cells == own_target.astype(jnp.float32)).astype(jnp.float32)[:, None, None],
        row_fields.shape[1:],
    )
    solved = bottom_solve(row_fields[0] * inside, row_fields[1] * inside, inside)
    bottom_corr = lax.dynamic_slice_in_dim(solved, lax.axis_index("gx") * cells_x, cells_x, 0)
    mid_sol = mid_sol + prolong(bottom_corr)
    mid_sol = relax_cells(coarse_halo(mid_sol), mid_pad, mid_src, 0.25, 0.0)
    mid_sol = relax_cells(coarse_halo(mid_sol), mid_pad, mid_src, 0.25, 0.0)
    fine_sol = fine_sol + prolong(mid_sol)
    fine_sol = relax_cells(post_halo(fine_sol), fine_pad, source, 1.0, 0.0)
    fine_sol = relax_cells(post_halo(fine_sol), fine_pad, source, 1.0, 0.0)
    return fine_sol


def solution(mesh):
    in_specs = (P("gx", "gy", "gz"), P("gx", "gy", "gz"), P("gx", "gy", "gz"))
    out_specs = P("gx", "gy", "gz")
    return jax.shard_map(
        per_device, mesh=mesh, in_specs=in_specs, out_specs=out_specs, check_vma=False
    )
```

profile of v0, /device:TPU:25, one launch (start us, length us, event | category | flops | bytes accessed | tf_op | source)
XLA Modules:
  0.0 337.5 jit_solution(9096053864388018885)
XLA Ops:
  12.1 4.3 %collective-permute-start.3 = (f32[10,1,128]{2,1,0:T(1,128)S(1)}, f32[10,1,128]{2,1,0:T(1,128)S(1)}, u32[]{:S(2)}, u32[]{:S(2)}) collective-permute-start(f32[10,1,128]{2,1,0:T(1,128)S(1)} %get-tuple-element.44), channel_id=1, source_target_pairs={{2,0},{4,2},{6,4},{8,6},{10,8},{12,10},{14,12},{16,14},{18,16},{20... | collective-permute-start | bytes 15368 | tf_op jit(solution)/shard_map/ppermute | solution.py:20
  18.6 5.0 %collective-permute-start.5 = (f32[10,34,1]{2,1,0:T(8,128)S(1)}, f32[10,34,1]{2,1,0:T(8,128)S(1)}, u32[]{:S(2)}, u32[]{:S(2)}) collective-permute-start(f32[10,34,1]{2,1,0:T(8,128)S(1)} %get-tuple-element.34), channel_id=1, source_target_pairs={{1,0},{3,2},{5,4},{7,6},{9,8},{11,10},{13,12},{15,14},{17,16},{19,... | collective-permute-start | bytes 4088 | tf_op jit(solution)/shard_map/ppermute | solution.py:20
  31.0 10.5 %reshape.67 = f32[4,2,16,2,64,2]{5,4,3,2,1,0:T(8,128)} reshape(f32[8,32,128]{2,1,0:T(8,128)} %param.4) | data formatting | bytes 262144 | tf_op jit(solution)/shard_map/reshape | solution.py:64
  48.4 5.2 %collective-permute-start.9 = (f32[10,1,128]{2,1,0:T(1,128)S(1)}, f32[10,1,128]{2,1,0:T(1,128)S(1)}, u32[]{:S(2)}, u32[]{:S(2)}) collective-permute-start(f32[10,1,128]{2,1,0:T(1,128)S(1)} %get-tuple-element.42), channel_id=1, source_target_pairs={{2,0},{4,2},{6,4},{8,6},{10,8},{12,10},{14,12},{16,14},{18,16},{20... | collective-permute-start | bytes 15368 | tf_op jit(solution)/shard_map/ppermute | solution.py:20
  59.2 5.3 %collective-permute-start.18 = (f32[1,16,64]{2,1,0:T(8,128)S(1)}, f32[1,16,64]{2,1,0:T(8,128)S(1)}, u32[]{:S(2)}, u32[]{:S(2)}) collective-permute-start(f32[1,16,64]{2,1,0:T(8,128)S(1)} %get-tuple-element.84), channel_id=1, source_target_pairs={{0,32},{32,64},{64,96},{96,128},{128,160},{160,192},{192,224},{224... | collective-permute-start | bytes 12296 | tf_op jit(solution)/shard_map/ppermute | solution.py:19
  66.1 5.5 %collective-permute-start.12 = (f32[1,32,128]{2,1,0:T(8,128)S(1)}, f32[1,32,128]{2,1,0:T(8,128)S(1)}, u32[]{:S(2)}, u32[]{:S(2)}) collective-permute-start(f32[1,32,128]{2,1,0:T(8,128)S(1)} %get-tuple-element.49), channel_id=1, source_target_pairs={{0,32},{32,64},{64,96},{96,128},{128,160},{160,192},{192,224},{224... | collective-permute-start | bytes 49160 | tf_op jit(solution)/shard_map/ppermute | solution.py:19
  74.9 6.0 %collective-permute-start.21 = (f32[6,1,64]{2,1,0:T(1,128)S(1)}, f32[6,1,64]{2,1,0:T(1,128)S(1)}, u32[]{:S(2)}, u32[]{:S(2)}) collective-permute-start(f32[6,1,64]{2,1,0:T(1,128)S(1)} %get-tuple-element.74), channel_id=1, source_target_pairs={{2,0},{4,2},{6,4},{8,6},{10,8},{12,10},{14,12},{16,14},{18,16},{20... | collective-permute-start | bytes 4616 | tf_op jit(solution)/shard_map/ppermute | solution.py:20
  82.9 5.5 %collective-permute-start.15 = (f32[10,1,128]{2,1,0:T(1,128)S(1)}, f32[10,1,128]{2,1,0:T(1,128)S(1)}, u32[]{:S(2)}, u32[]{:S(2)}) collective-permute-start(f32[10,1,128]{2,1,0:T(1,128)S(1)} %get-tuple-element.40), channel_id=1, source_target_pairs={{2,0},{4,2},{6,4},{8,6},{10,8},{12,10},{14,12},{16,14},{18,16},{20... | collective-permute-start | bytes 15368 | tf_op jit(solution)/shard_map/ppermute | solution.py:20
  98.5 9.8 %reshape.66 = f32[4,2,16,2,64,2]{5,4,3,2,1,0:T(8,128)} reshape(f32[8,32,128]{2,1,0:T(8,128)S(1)} %fusion.205) | data formatting | bytes 262144 | tf_op jit(solution)/shard_map/reshape | solution.py:64
  112.5 4.3 %collective-permute-start.24 = (f32[1,16,64]{2,1,0:T(8,128)S(1)}, f32[1,16,64]{2,1,0:T(8,128)S(1)}, u32[]{:S(2)}, u32[]{:S(2)}) collective-permute-start(f32[1,16,64]{2,1,0:T(8,128)S(1)} %get-tuple-element.81), channel_id=1, source_target_pairs={{0,32},{32,64},{64,96},{96,128},{128,160},{160,192},{192,224},{224... | collective-permute-start | bytes 12296 | tf_op jit(solution)/shard_map/ppermute | solution.py:19
  123.5 6.0 %collective-permute-start.27 = (f32[6,1,64]{2,1,0:T(1,128)S(1)}, f32[6,1,64]{2,1,0:T(1,128)S(1)}, u32[]{:S(2)}, u32[]{:S(2)}) collective-permute-start(f32[6,1,64]{2,1,0:T(1,128)S(1)} %get-tuple-element.72), channel_id=1, source_target_pairs={{2,0},{4,2},{6,4},{8,6},{10,8},{12,10},{14,12},{16,14},{18,16},{20... | collective-permute-start | bytes 4616 | tf_op jit(solution)/shard_map/ppermute | solution.py:20
  136.8 29.6 %all-reduce.9 = f32[16]{0:T(128)S(1)} all-reduce(f32[16]{0:T(128)S(1)} %bitcast_dynamic-update-slice_fusion), channel_id=1, replica_groups=mesh['gx'=16,'gy'=16,'gz'=2] {'gx'}, use_global_device_ids=true, to_apply=%add.9 | all-reduce | flops 16 | bytes 128
  174.2 6.0 %collective-permute-start.33 = (f32[6,1,64]{2,1,0:T(1,128)S(1)}, f32[6,1,64]{2,1,0:T(1,128)S(1)}, u32[]{:S(2)}, u32[]{:S(2)}) collective-permute-start(f32[6,1,64]{2,1,0:T(1,128)S(1)} %get-tuple-element.70), channel_id=1, source_target_pairs={{2,0},{4,2},{6,4},{8,6},{10,8},{12,10},{14,12},{16,14},{18,16},{20... | collective-permute-start | bytes 4616 | tf_op jit(solution)/shard_map/ppermute | solution.py:20
  182.9 9.4 %collective-permute-start.35 = (f32[6,18,1]{2,1,0:T(8,128)S(1)}, f32[6,18,1]{2,1,0:T(8,128)S(1)}, u32[]{:S(2)}, u32[]{:S(2)}) collective-permute-start(f32[6,18,1]{2,1,0:T(8,128)S(1)} %get-tuple-element.60), channel_id=1, source_target_pairs={{1,0},{3,2},{5,4},{7,6},{9,8},{11,10},{13,12},{15,14},{17,16},{19,... | collective-permute-start | bytes 1304 | tf_op jit(solution)/shard_map/ppermute | solution.py:20
  194.6 25.3 %all_gather.7 = f32[2,32,8,32]{3,2,1,0:T(8,128)S(1)} all-gather(f32[2,2,8,32]{3,2,1,0:T(8,128)S(1)} %pad_maximum_fusion.182), channel_id=1, replica_groups=mesh['gx'=16,'gy'=16,'gz'=2] {'gx'}, dimensions={1}, use_global_device_ids=true | all-gather | bytes 69632 | tf_op jit(solution)/shard_map/all_gather | solution.py:113
  232.1 6.0 %collective-permute-start.39 = (f32[6,1,64]{2,1,0:T(1,128)S(1)}, f32[6,1,64]{2,1,0:T(1,128)S(1)}, u32[]{:S(2)}, u32[]{:S(2)}) collective-permute-start(f32[6,1,64]{2,1,0:T(1,128)S(1)} %get-tuple-element.68), channel_id=1, source_target_pairs={{2,0},{4,2},{6,4},{8,6},{10,8},{12,10},{14,12},{16,14},{18,16},{20... | collective-permute-start | bytes 4616 | tf_op jit(solution)/shard_map/ppermute | solution.py:20
  240.2 11.6 %collective-permute-start.41 = (f32[6,18,1]{2,1,0:T(8,128)S(1)}, f32[6,18,1]{2,1,0:T(8,128)S(1)}, u32[]{:S(2)}, u32[]{:S(2)}) collective-permute-start(f32[6,18,1]{2,1,0:T(8,128)S(1)} %get-tuple-element.58), channel_id=1, source_target_pairs={{1,0},{3,2},{5,4},{7,6},{9,8},{11,10},{13,12},{15,14},{17,16},{19,... | collective-permute-start | bytes 1304 | tf_op jit(solution)/shard_map/ppermute | solution.py:20
  263.0 6.0 %collective-permute-start.45 = (f32[6,1,64]{2,1,0:T(1,128)S(1)}, f32[6,1,64]{2,1,0:T(1,128)S(1)}, u32[]{:S(2)}, u32[]{:S(2)}) collective-permute-start(f32[6,1,64]{2,1,0:T(1,128)S(1)} %get-tuple-element.66), channel_id=1, source_target_pairs={{2,0},{4,2},{6,4},{8,6},{10,8},{12,10},{14,12},{16,14},{18,16},{20... | collective-permute-start | bytes 4616 | tf_op jit(solution)/shard_map/ppermute | solution.py:20
  280.4 6.9 %reshape.70 = f32[8,32,128]{2,1,0:T(8,128)S(1)} reshape(f32[4,2,16,2,64,2]{5,4,3,2,1,0:T(8,128)} %broadcast_in_dim.43) | data formatting | bytes 262144 | tf_op jit(solution)/shard_map/reshape | solution.py:70
  287.3 4.8 %collective-permute-start.48 = (f32[1,32,128]{2,1,0:T(8,128)S(1)}, f32[1,32,128]{2,1,0:T(8,128)S(1)}, u32[]{:S(2)}, u32[]{:S(2)}) collective-permute-start(f32[1,32,128]{2,1,0:T(8,128)S(1)} %get-tuple-element.47), channel_id=1, source_target_pairs={{0,32},{32,64},{64,96},{96,128},{128,160},{160,192},{192,224},{224... | collective-permute-start | bytes 49160 | tf_op jit(solution)/shard_map/ppermute | solution.py:19
  298.9 6.0 %collective-permute-start.51 = (f32[10,1,128]{2,1,0:T(1,128)S(1)}, f32[10,1,128]{2,1,0:T(1,128)S(1)}, u32[]{:S(2)}, u32[]{:S(2)}) collective-permute-start(f32[10,1,128]{2,1,0:T(1,128)S(1)} %get-tuple-element.38), channel_id=1, source_target_pairs={{2,0},{4,2},{6,4},{8,6},{10,8},{12,10},{14,12},{16,14},{18,16},{20... | collective-permute-start | bytes 15368 | tf_op jit(solution)/shard_map/ppermute | solution.py:20
  307.1 4.3 %collective-permute-start.53 = (f32[10,34,1]{2,1,0:T(8,128)S(1)}, f32[10,34,1]{2,1,0:T(8,128)S(1)}, u32[]{:S(2)}, u32[]{:S(2)}) collective-permute-start(f32[10,34,1]{2,1,0:T(8,128)S(1)} %get-tuple-element.28), channel_id=1, source_target_pairs={{1,0},{3,2},{5,4},{7,6},{9,8},{11,10},{13,12},{15,14},{17,16},{19,... | collective-permute-start | bytes 4088 | tf_op jit(solution)/shard_map/ppermute | solution.py:20
  322.7 6.0 %collective-permute-start.57 = (f32[10,1,128]{2,1,0:T(1,128)S(1)}, f32[10,1,128]{2,1,0:T(1,128)S(1)}, u32[]{:S(2)}, u32[]{:S(2)}) collective-permute-start(f32[10,1,128]{2,1,0:T(1,128)S(1)} %get-tuple-element.36), channel_id=1, source_target_pairs={{2,0},{4,2},{6,4},{8,6},{10,8},{12,10},{14,12},{16,14},{18,16},{20... | collective-permute-start | bytes 15368 | tf_op jit(solution)/shard_map/ppermute | solution.py:20
  331.0 4.6 %collective-permute-start.59 = (f32[10,34,1]{2,1,0:T(8,128)S(1)}, f32[10,34,1]{2,1,0:T(8,128)S(1)}, u32[]{:S(2)}, u32[]{:S(2)}) collective-permute-start(f32[10,34,1]{2,1,0:T(8,128)S(1)} %get-tuple-element.26), channel_id=1, source_target_pairs={{1,0},{3,2},{5,4},{7,6},{9,8},{11,10},{13,12},{15,14},{17,16},{19,... | collective-permute-start | bytes 4088 | tf_op jit(solution)/shard_map/ppermute | solution.py:20
  (195 shorter events, 140.4 us)
Async XLA Ops:
  26.0 19.6 %collective-permute-start.6 = (f32[1,32,128]{2,1,0:T(8,128)S(1)}, f32[1,32,128]{2,1,0:T(8,128)S(1)}, u32[]{:S(2)}, u32[]{:S(2)}) collective-permute-start(f32[1,32,128]{2,1,0:T(8,128)S(1)} %get-tuple-element.51), channel_id=1, source_target_pairs={{0,32},{32,64},{64,96},{96,128},{128,160},{160,192},{192,224},{224... | collective-permute-start | bytes 49160 | tf_op jit(solution)/shard_map/ppermute | solution.py:19
  29.6 16.0 %collective-permute-start.7 = (f32[1,32,128]{2,1,0:T(8,128)S(1)}, f32[1,32,128]{2,1,0:T(8,128)S(1)}, u32[]{:S(2)}, u32[]{:S(2)}) collective-permute-start(f32[1,32,128]{2,1,0:T(8,128)S(1)} %get-tuple-element.52), channel_id=1, source_target_pairs={{32,0},{64,32},{96,64},{128,96},{160,128},{192,160},{224,192},{256... | collective-permute-start | bytes 49160 | tf_op jit(solution)/shard_map/ppermute | solution.py:20
  45.6 8.0 %collective-permute-start.8 = (f32[10,1,128]{2,1,0:T(1,128)S(1)}, f32[10,1,128]{2,1,0:T(1,128)S(1)}, u32[]{:S(2)}, u32[]{:S(2)}) collective-permute-start(f32[10,1,128]{2,1,0:T(1,128)S(1)} %get-tuple-element.41), channel_id=1, source_target_pairs={{0,2},{2,4},{4,6},{6,8},{8,10},{10,12},{12,14},{14,16},{16,18},{18... | collective-permute-start | bytes 15368 | tf_op jit(solution)/shard_map/ppermute | solution.py:19
  54.5 11.4 %collective-permute-start.10 = (f32[10,34,1]{2,1,0:T(8,128)S(1)}, f32[10,34,1]{2,1,0:T(8,128)S(1)}, u32[]{:S(2)}, u32[]{:S(2)}) collective-permute-start(f32[10,34,1]{2,1,0:T(8,128)S(1)} %get-tuple-element.31), channel_id=1, source_target_pairs={{0,1},{2,3},{4,5},{6,7},{8,9},{10,11},{12,13},{14,15},{16,17},{18,... | collective-permute-start | bytes 4088 | tf_op jit(solution)/shard_map/ppermute | solution.py:19
  55.8 10.1 %collective-permute-start.11 = (f32[10,34,1]{2,1,0:T(8,128)S(1)}, f32[10,34,1]{2,1,0:T(8,128)S(1)}, u32[]{:S(2)}, u32[]{:S(2)}) collective-permute-start(f32[10,34,1]{2,1,0:T(8,128)S(1)} %get-tuple-element.32), channel_id=1, source_target_pairs={{1,0},{3,2},{5,4},{7,6},{9,8},{11,10},{13,12},{15,14},{17,16},{19,... | collective-permute-start | bytes 4088 | tf_op jit(solution)/shard_map/ppermute | solution.py:20
  59.2 13.7 %collective-permute-start.18 = (f32[1,16,64]{2,1,0:T(8,128)S(1)}, f32[1,16,64]{2,1,0:T(8,128)S(1)}, u32[]{:S(2)}, u32[]{:S(2)}) collective-permute-start(f32[1,16,64]{2,1,0:T(8,128)S(1)} %get-tuple-element.84), channel_id=1, source_target_pairs={{0,32},{32,64},{64,96},{96,128},{128,160},{160,192},{192,224},{224... | collective-permute-start | bytes 12296 | tf_op jit(solution)/shard_map/ppermute | solution.py:19
  64.5 8.4 %collective-permute-start.19 = (f32[1,16,64]{2,1,0:T(8,128)S(1)}, f32[1,16,64]{2,1,0:T(8,128)S(1)}, u32[]{:S(2)}, u32[]{:S(2)}) collective-permute-start(f32[1,16,64]{2,1,0:T(8,128)S(1)} %get-tuple-element.83), channel_id=1, source_target_pairs={{32,0},{64,32},{96,64},{128,96},{160,128},{192,160},{224,192},{256... | collective-permute-start | bytes 12296 | tf_op jit(solution)/shard_map/ppermute | solution.py:20
  66.1 14.8 %collective-permute-start.12 = (f32[1,32,128]{2,1,0:T(8,128)S(1)}, f32[1,32,128]{2,1,0:T(8,128)S(1)}, u32[]{:S(2)}, u32[]{:S(2)}) collective-permute-start(f32[1,32,128]{2,1,0:T(8,128)S(1)} %get-tuple-element.49), channel_id=1, source_target_pairs={{0,32},{32,64},{64,96},{96,128},{128,160},{160,192},{192,224},{224... | collective-permute-start | bytes 49160 | tf_op jit(solution)/shard_map/ppermute | solution.py:19
  71.6 9.3 %collective-permute-start.13 = (f32[1,32,128]{2,1,0:T(8,128)S(1)}, f32[1,32,128]{2,1,0:T(8,128)S(1)}, u32[]{:S(2)}, u32[]{:S(2)}) collective-permute-start(f32[1,32,128]{2,1,0:T(8,128)S(1)} %get-tuple-element.50), channel_id=1, source_target_pairs={{32,0},{64,32},{96,64},{128,96},{160,128},{192,160},{224,192},{256... | collective-permute-start | bytes 49160 | tf_op jit(solution)/shard_map/ppermute | solution.py:20
  72.9 15.4 %collective-permute-start.20 = (f32[6,1,64]{2,1,0:T(1,128)S(1)}, f32[6,1,64]{2,1,0:T(1,128)S(1)}, u32[]{:S(2)}, u32[]{:S(2)}) collective-permute-start(f32[6,1,64]{2,1,0:T(1,128)S(1)} %get-tuple-element.73), channel_id=1, source_target_pairs={{0,2},{2,4},{4,6},{6,8},{8,10},{10,12},{12,14},{14,16},{16,18},{18... | collective-permute-start | bytes 4616 | tf_op jit(solution)/shard_map/ppermute | solution.py:19
  74.9 13.5 %collective-permute-start.21 = (f32[6,1,64]{2,1,0:T(1,128)S(1)}, f32[6,1,64]{2,1,0:T(1,128)S(1)}, u32[]{:S(2)}, u32[]{:S(2)}) collective-permute-start(f32[6,1,64]{2,1,0:T(1,128)S(1)} %get-tuple-element.74), channel_id=1, source_target_pairs={{2,0},{4,2},{6,4},{8,6},{10,8},{12,10},{14,12},{16,14},{18,16},{20... | collective-permute-start | bytes 4616 | tf_op jit(solution)/shard_map/ppermute | solution.py:20
  89.2 9.0 %collective-permute-start.16 = (f32[10,34,1]{2,1,0:T(8,128)S(1)}, f32[10,34,1]{2,1,0:T(8,128)S(1)}, u32[]{:S(2)}, u32[]{:S(2)}) collective-permute-start(f32[10,34,1]{2,1,0:T(8,128)S(1)} %get-tuple-element.29), channel_id=1, source_target_pairs={{0,1},{2,3},{4,5},{6,7},{8,9},{10,11},{12,13},{14,15},{16,17},{18,... | collective-permute-start | bytes 4088 | tf_op jit(solution)/shard_map/ppermute | solution.py:19
  93.9 18.4 %collective-permute-start.22 = (f32[6,18,1]{2,1,0:T(8,128)S(1)}, f32[6,18,1]{2,1,0:T(8,128)S(1)}, u32[]{:S(2)}, u32[]{:S(2)}) collective-permute-start(f32[6,18,1]{2,1,0:T(8,128)S(1)} %get-tuple-element.63), channel_id=1, source_target_pairs={{0,1},{2,3},{4,5},{6,7},{8,9},{10,11},{12,13},{14,15},{16,17},{18,... | collective-permute-start | bytes 1304 | tf_op jit(solution)/shard_map/ppermute | solution.py:19
  95.2 17.1 %collective-permute-start.23 = (f32[6,18,1]{2,1,0:T(8,128)S(1)}, f32[6,18,1]{2,1,0:T(8,128)S(1)}, u32[]{:S(2)}, u32[]{:S(2)}) collective-permute-start(f32[6,18,1]{2,1,0:T(8,128)S(1)} %get-tuple-element.64), channel_id=1, source_target_pairs={{1,0},{3,2},{5,4},{7,6},{9,8},{11,10},{13,12},{15,14},{17,16},{19,... | collective-permute-start | bytes 1304 | tf_op jit(solution)/shard_map/ppermute | solution.py:20
  121.6 8.6 %collective-permute-start.26 = (f32[6,1,64]{2,1,0:T(1,128)S(1)}, f32[6,1,64]{2,1,0:T(1,128)S(1)}, u32[]{:S(2)}, u32[]{:S(2)}) collective-permute-start(f32[6,1,64]{2,1,0:T(1,128)S(1)} %get-tuple-element.71), channel_id=1, source_target_pairs={{0,2},{2,4},{4,6},{6,8},{8,10},{10,12},{12,14},{14,16},{16,18},{18... | collective-permute-start | bytes 4616 | tf_op jit(solution)/shard_map/ppermute | solution.py:19
  130.3 36.1 %collective-permute-start.28 = (f32[6,18,1]{2,1,0:T(8,128)S(1)}, f32[6,18,1]{2,1,0:T(8,128)S(1)}, u32[]{:S(2)}, u32[]{:S(2)}) collective-permute-start(f32[6,18,1]{2,1,0:T(8,128)S(1)} %get-tuple-element.61), channel_id=1, source_target_pairs={{0,1},{2,3},{4,5},{6,7},{8,9},{10,11},{12,13},{14,15},{16,17},{18,... | collective-permute-start | bytes 1304 | tf_op jit(solution)/shard_map/ppermute | solution.py:19
  131.6 34.8 %collective-permute-start.29 = (f32[6,18,1]{2,1,0:T(8,128)S(1)}, f32[6,18,1]{2,1,0:T(8,128)S(1)}, u32[]{:S(2)}, u32[]{:S(2)}) collective-permute-start(f32[6,18,1]{2,1,0:T(8,128)S(1)} %get-tuple-element.62), channel_id=1, source_target_pairs={{1,0},{3,2},{5,4},{7,6},{9,8},{11,10},{13,12},{15,14},{17,16},{19,... | collective-permute-start | bytes 1304 | tf_op jit(solution)/shard_map/ppermute | solution.py:20
  172.3 9.2 %collective-permute-start.32 = (f32[6,1,64]{2,1,0:T(1,128)S(1)}, f32[6,1,64]{2,1,0:T(1,128)S(1)}, u32[]{:S(2)}, u32[]{:S(2)}) collective-permute-start(f32[6,1,64]{2,1,0:T(1,128)S(1)} %get-tuple-element.69), channel_id=1, source_target_pairs={{0,2},{2,4},{4,6},{6,8},{8,10},{10,12},{12,14},{14,16},{16,18},{18... | collective-permute-start | bytes 4616 | tf_op jit(solution)/shard_map/ppermute | solution.py:19
  181.6 10.8 %collective-permute-start.34 = (f32[6,18,1]{2,1,0:T(8,128)S(1)}, f32[6,18,1]{2,1,0:T(8,128)S(1)}, u32[]{:S(2)}, u32[]{:S(2)}) collective-permute-start(f32[6,18,1]{2,1,0:T(8,128)S(1)} %get-tuple-element.59), channel_id=1, source_target_pairs={{0,1},{2,3},{4,5},{6,7},{8,9},{10,11},{12,13},{14,15},{16,17},{18,... | collective-permute-start | bytes 1304 | tf_op jit(solution)/shard_map/ppermute | solution.py:19
  182.9 10.3 %collective-permute-start.35 = (f32[6,18,1]{2,1,0:T(8,128)S(1)}, f32[6,18,1]{2,1,0:T(8,128)S(1)}, u32[]{:S(2)}, u32[]{:S(2)}) collective-permute-start(f32[6,18,1]{2,1,0:T(8,128)S(1)} %get-tuple-element.60), channel_id=1, source_target_pairs={{1,0},{3,2},{5,4},{7,6},{9,8},{11,10},{13,12},{15,14},{17,16},{19,... | collective-permute-start | bytes 1304 | tf_op jit(solution)/shard_map/ppermute | solution.py:20
  230.2 8.0 %collective-permute-start.38 = (f32[6,1,64]{2,1,0:T(1,128)S(1)}, f32[6,1,64]{2,1,0:T(1,128)S(1)}, u32[]{:S(2)}, u32[]{:S(2)}) collective-permute-start(f32[6,1,64]{2,1,0:T(1,128)S(1)} %get-tuple-element.67), channel_id=1, source_target_pairs={{0,2},{2,4},{4,6},{6,8},{8,10},{10,12},{12,14},{14,16},{16,18},{18... | collective-permute-start | bytes 4616 | tf_op jit(solution)/shard_map/ppermute | solution.py:19
  238.9 12.9 %collective-permute-start.40 = (f32[6,18,1]{2,1,0:T(8,128)S(1)}, f32[6,18,1]{2,1,0:T(8,128)S(1)}, u32[]{:S(2)}, u32[]{:S(2)}) collective-permute-start(f32[6,18,1]{2,1,0:T(8,128)S(1)} %get-tuple-element.57), channel_id=1, source_target_pairs={{0,1},{2,3},{4,5},{6,7},{8,9},{10,11},{12,13},{14,15},{16,17},{18,... | collective-permute-start | bytes 1304 | tf_op jit(solution)/shard_map/ppermute | solution.py:19
  240.2 12.5 %collective-permute-start.41 = (f32[6,18,1]{2,1,0:T(8,128)S(1)}, f32[6,18,1]{2,1,0:T(8,128)S(1)}, u32[]{:S(2)}, u32[]{:S(2)}) collective-permute-start(f32[6,18,1]{2,1,0:T(8,128)S(1)} %get-tuple-element.58), channel_id=1, source_target_pairs={{1,0},{3,2},{5,4},{7,6},{9,8},{11,10},{13,12},{15,14},{17,16},{19,... | collective-permute-start | bytes 1304 | tf_op jit(solution)/shard_map/ppermute | solution.py:20
  320.8 8.0 %collective-permute-start.56 = (f32[10,1,128]{2,1,0:T(1,128)S(1)}, f32[10,1,128]{2,1,0:T(1,128)S(1)}, u32[]{:S(2)}, u32[]{:S(2)}) collective-permute-start(f32[10,1,128]{2,1,0:T(1,128)S(1)} %get-tuple-element.35), channel_id=1, source_target_pairs={{0,2},{2,4},{4,6},{6,8},{8,10},{10,12},{12,14},{14,16},{16,18},{18... | collective-permute-start | bytes 15368 | tf_op jit(solution)/shard_map/ppermute | solution.py:19
  (38 other events, 278.7 us)
where the time goes:
time: 341 us; the launch traced here: 337 us
  starting transfers between devices  192 us (56%)
  blocking collectives  55 us (16%)
  local copies, waits for them, and re-layouts  39.3 us (12%)
  waiting for transfers between devices  33.3 us (10%)
  other arithmetic  14.4 us (4%)
    ppermute x30, starting transfers between devices, padded(): after = lax.ppermute(first, axis, down)  122 us
    ppermute x30, starting transfers between devices, padded(): before = lax.ppermute(last, axis, up)  70.3 us
    ppermute x30, waiting for transfers between devices, padded(): after = lax.ppermute(first, axis, down)  33.2 us
    unnamed x1, blocking collectives  29.6 us
    all_gather x1, blocking collectives, per_device(): lax.all_gather(jnp.stack([low_src, low_coef]), 'gx', axis=1, tiled=True)  25.3 us
    reshape x3, local copies, waits for them, and re-layouts, restrict(): field.reshape(size_a // 2, 2, size_b // 2, 2, size_c // 2, 2)  21.4 us
    reduce_sum x4, other arithmetic, restrict(): field.reshape(size_a // 2, 2, size_b // 2, 2, size_c // 2, 2)  8.32 us
    reshape x2, local copies, waits for them, and re-layouts, prolong(): return spread.reshape(2 * size_a, 2 * size_b, 2 * size_c)  7.54 us
  transfers between devices with their start and end apart: 60, of which 21 were waited for; matrix products, arithmetic and copies ran while one was open for 10% of the time, Pallas kernels for 0%

commit v1 on v0

v1 whole, which is shorter than its diff:
```python
import jax
import jax.numpy as jnp
from jax import lax
from jax.experimental import pallas as pl
from jax.experimental.pallas import tpu as pltpu
from jax.sharding import PartitionSpec as P


BOTTOM = 6
RELAX = 0.8
F32 = jnp.float32
MESH = pl.DeviceIdType.MESH
NEAR = 4


def lanes_of(rows):
    return lax.broadcasted_iota(jnp.int32, (rows, 128), 1)


def beside(left_tile, right_tile, step):
    lane = lanes_of(left_tile.shape[0])
    low0, low1 = pltpu.roll(left_tile, step, 1), pltpu.roll(right_tile, step, 1)
    high0, high1 = pltpu.roll(left_tile, 128 - step, 1), pltpu.roll(right_tile, 128 - step, 1)
    below = (low0, jnp.where(lane < step, low0, low1))
    above = (jnp.where(lane >= 128 - step, high1, high0), high1)
    return below, above


def make_faces(x, coef, faces, row, rows, step):
    fx, fy, fl, fr, weight, ease = faces
    at = pl.ds(row, rows)
    own = [coef[x, t, at, :] for t in range(2)]
    below, above = beside(*own, step)
    lane = lanes_of(rows)
    for t in range(2):
        c = own[t]
        low = jnp.where(lane < step, 0.0, below[0]) if t == 0 else below[1]
        high = jnp.where(lane >= 128 - step, 0.0, above[1]) if t == 1 else above[0]
        x_low = c + coef[x - 1, t, at, :]
        y_low = c + coef[x, t, pl.ds(row - 1, rows), :]
        z_low, z_high = c + low, c + high
        total = (
            x_low
            + (c + coef[x + 1, t, at, :])
            + y_low
            + (c + coef[x, t, pl.ds(row + 1, rows), :])
            + z_low
            + z_high
        )
        fx[x, t, at, :] = x_low
        fy[x, t, at, :] = y_low
        fl[x, t, at, :] = jnp.where(lane < step, 0.0, z_low) if t == 0 else z_low
        fr[x, t, at, :] = jnp.where(lane >= 128 - step, 0.0, z_high) if t == 1 else z_high
        weight[x, t, at, :] = total
        ease[x, t, at, :] = jnp.where(c > 0.0, RELAX / total, 0.0)


def last_face(x, coef, faces, row, rows):
    at = pl.ds(row, rows)
    for t in range(2):
        faces[0][x, t, at, :] = coef[x, t, at, :] + coef[x - 1, t, at, :]


def pull(x, field, faces, row, rows, step):
    fx, fy, fl, fr = faces[:4]
    at = pl.ds(row, rows)
    own = [field[x, t, at, :] for t in range(2)]
    below, above = beside(*own, step)
    sums = []
    for t in range(2):
        sums.append(
            fx[x, t, at, :] * field[x - 1, t, at, :]
            + fx[x + 1, t, at, :] * field[x + 1, t, at, :]
            + fy[x, t, at, :] * field[x, t, pl.ds(row - 1, rows), :]
            + fy[x, t, pl.ds(row + 1, rows), :] * field[x, t, pl.ds(row + 1, rows), :]
            + fl[x, t, at, :] * below[t]
            + fr[x, t, at, :] * above[t]
        )
    return sums, own


def sweep(x, field, out, faces, source, gain, row, rows, step):
    at = pl.ds(row, rows)
    sums, own = pull(x, field, faces, row, rows, step)
    for t in range(2):
        out[x, t, at, :] = 0.2 * own[t] + faces[5][x, t, at, :] * (gain * source[x, t, at, :] + sums[t])


def left_over(x, field, faces, source, half, row, rows, step):
    at = pl.ds(row, rows)
    sums, own = pull(x, field, faces, row, rows, step)
    return [source[x, t, at, :] - half * (faces[4][x, t, at, :] * own[t] - sums[t]) for t in range(2)]


def pair_sum(value, step):
    lane = lanes_of(value.shape[0])
    other = jnp.where((lane // step) % 2 == 0, pltpu.roll(value, 128 - step, 1), pltpu.roll(value, step, 1))
    return value + other


def exact_dot(a, b):
    return jnp.dot(a, b, precision=lax.Precision.HIGHEST, preferred_element_type=F32)


def squeeze_matrix(part):
    src = lax.broadcasted_iota(jnp.int32, (128, 128), 0)
    dst = lax.broadcasted_iota(jnp.int32, (128, 128), 1)
    return jnp.where((src == 4 * (dst % 32)) & (dst // 32 == part), 1.0, 0.0).astype(F32)


def spread_matrix(part):
    src = lax.broadcasted_iota(jnp.int32, (128, 128), 0)
    dst = lax.broadcasted_iota(jnp.int32, (128, 128), 1)
    return jnp.where(src == 32 * part + dst // 4, 1.0, 0.0).astype(F32)


def cycle(n_gx, n_gy, src, beta, tgt, out, *scratch):
    (C, S, FX, FY, FL, FR, W, E, V1, V2, V3,
     MC, MS, MFX, MFY, MFL, MFR, MW, ME, M1, M2, M2P, M3, M4,
     RS, RC, R2, SY, Y2, SX, EB, ES, GB, GS, FB, FS, Q, SQ, PK, PF, FO,
     local, e1s, e1r, mcs, mcr, mss, msr, ebs, ebr, gs, gr, fs, fr, ys, yr, xs, xr, qs, qr, os_, or_) = scratch
    i, j, g = lax.axis_index("gx"), lax.axis_index("gy"), lax.axis_index("gz")
    fine = (FX, FY, FL, FR, W, E)
    mid = (MFX, MFY, MFL, MFR, MW, ME)

    def near_x(d):
        return lax.rem(i + d + n_gx, n_gx)

    def near_y(d):
        return lax.rem(j + d + n_gy, n_gy)

    def send(source, target, send_sem, recv_sem, where):
        pltpu.make_async_remote_copy(
            src_ref=source, dst_ref=target, send_sem=send_sem, recv_sem=recv_sem,
            device_id=where, device_id_type=MESH,
        ).start()

    def wait(ref, sem):
        pltpu.make_async_copy(ref, ref, sem).wait()

    own_rows = pl.ds(pl.multiple_of(8 * g, 8), 24)
    own_at = pl.ds(pl.multiple_of(16 - 8 * g, 8), 24)
    pltpu.make_async_copy(beta.at[:, own_rows, :], C.at[pl.ds(4, 8), g, own_at, :], local.at[0]).start()
    pltpu.make_async_copy(src.at[:, own_rows, :], S.at[pl.ds(4, 8), g, own_at, :], local.at[1]).start()

    barrier = pltpu.get_barrier_semaphore()
    side = 2 * g - 1
    count = 0
    for d in range(1, n_gx):
        for core in range(2):
            pl.semaphore_signal(barrier, inc=1, device_id=(near_x(d), j, core), device_id_type=MESH)
            count += 1
    for dx in (-1, 0, 1):
        for core in range(2):
            pl.semaphore_signal(barrier, inc=1, device_id=(near_x(dx), near_y(side), core), device_id_type=MESH)
            count += 1
    pl.semaphore_signal(barrier, inc=1, device_id=(i, j, 1 - g), device_id_type=MESH)
    pl.semaphore_wait(barrier, count + 1)

    for index, (field, target, deep) in enumerate(((beta, C, 4), (src, S, 3))):
        ss, rs = e1s.at[index], e1r.at[index]
        for dx in (1, -1):
            part = pl.ds(8 - deep, deep) if dx == 1 else pl.ds(0, deep)
            place = pl.ds(4 - deep, deep) if dx == 1 else pl.ds(12, deep)
            for core in range(2):
                dy = 1 if core == 0 else -1
                send(field.at[part, pl.ds(24 if core == 0 else 0, 8), :],
                     target.at[place, g, pl.ds(8 if core == 0 else 32, 8), :], ss, rs,
                     (near_x(dx), near_y(dy), core))
                send(field.at[part, pl.ds(8 * core, 24), :],
                     target.at[place, g, pl.ds(16 - 8 * core, 24), :], ss, rs, (near_x(dx), j, core))
        for core in range(2):
            dy = 1 if core == 0 else -1
            send(field.at[:, pl.ds(24 if core == 0 else 0, 8), :],
                 target.at[pl.ds(4, 8), g, pl.ds(8 if core == 0 else 32, 8), :], ss, rs, (i, near_y(dy), core))
        send(field.at[:, pl.ds(pl.multiple_of(8 - 8 * g, 8), 24), :],
             target.at[pl.ds(4, 8), g, pl.ds(pl.multiple_of(8 + 8 * g, 8), 24), :], ss, rs, (i, j, 1 - g))

    c_bytes = C.at[pl.ds(0, 13), :, pl.ds(0, 32), :]
    s_bytes = S.at[pl.ds(0, 11), :, pl.ds(0, 32), :]
    wait(beta.at[:, pl.ds(0, 24), :], local.at[0])
    wait(c_bytes, e1r.at[0])

    @pl.when(i == 0)
    def _():
        C[pl.ds(0, 4)] = jnp.zeros((4, *C.shape[1:]), F32)

    @pl.when(i == n_gx - 1)
    def _():
        C[pl.ds(12, 4)] = jnp.zeros((4, *C.shape[1:]), F32)

    @pl.when((j == 0) & (g == 0))
    def _():
        C[:, :, pl.ds(8, 8), :] = jnp.zeros((16, 2, 8, 128), F32)

    @pl.when((j == n_gy - 1) & (g == 1))
    def _():
        C[:, :, pl.ds(32, 8), :] = jnp.zeros((16, 2, 8, 128), F32)

    def mid_coefficient(m, _):
        for t in range(2):
            RC[m, t] = C[4 + 2 * m, t, pl.ds(8, 32), :] + C[5 + 2 * m, t, pl.ds(8, 32), :]
            two = RC[m, t, pl.ds(0, 16, stride=2), :] + RC[m, t, pl.ds(1, 16, stride=2), :]
            MC[m + 3, t, pl.ds(8, 16), :] = 0.125 * pair_sum(two, 1)
        return 0

    lax.fori_loop(0, 4, mid_coefficient, 0)
    mid_rows = pl.ds(8, 16)
    send(MC.at[pl.ds(4, 3), :, mid_rows, :], MC.at[pl.ds(0, 3), :, mid_rows, :], mcs, mcr, (near_x(1), j, g))
    send(MC.at[pl.ds(3, 3), :, mid_rows, :], MC.at[pl.ds(7, 3), :, mid_rows, :], mcs, mcr, (near_x(-1), j, g))

    wait(src.at[:, pl.ds(0, 24), :], local.at[1])
    wait(s_bytes, e1r.at[1])

    def fine_first(x, _):
        make_faces(x, C, fine, 8, 32, 1)
        for t in range(2):
            V1[x, t, pl.ds(8, 32), :] = E[x, t, pl.ds(8, 32), :] * (2.0 * S[x, t, pl.ds(8, 32), :])
        return 0

    lax.fori_loop(1, 15, fine_first, 0)
    last_face(15, C, fine, 8, 32)

    def fine_second(x, _):
        sweep(x, V1, V2, fine, S, 2.0, 8, 32, 1)
        return 0

    lax.fori_loop(2, 14, fine_second, 0)

    def fine_residual(m, _):
        lower = left_over(4 + 2 * m, V2, fine, S, 0.5, 8, 32, 1)
        upper = left_over(5 + 2 * m, V2, fine, S, 0.5, 8, 32, 1)
        for t in range(2):
            RS[m, t] = lower[t] + upper[t]
            two = RS[m, t, pl.ds(0, 16, stride=2), :] + RS[m, t, pl.ds(1, 16, stride=2), :]
            MS[m + 3, t, mid_rows, :] = 0.125 * pair_sum(two, 1)
        return 0

    lax.fori_loop(0, 4, fine_residual, 0)
    send(MS.at[pl.ds(5, 2), :, mid_rows, :], MS.at[pl.ds(1, 2), :, mid_rows, :], mss, msr, (near_x(1), j, g))
    send(MS.at[pl.ds(3, 2), :, mid_rows, :], MS.at[pl.ds(7, 2), :, mid_rows, :], mss, msr, (near_x(-1), j, g))

    def squeeze(parts):
        total = None
        for part, value in enumerate(parts):
            term = exact_dot(value, squeeze_matrix(part))
            total = term if total is None else total + term
        return total

    def coarsest(field, scale):
        parts = []
        for layer in range(2):
            for t in range(2):
                R2[layer, t] = field(2 * layer, t) + field(2 * layer + 1, t)
                two = R2[layer, t, pl.ds(4, 4, stride=2), :] + R2[layer, t, pl.ds(5, 4, stride=2), :]
                parts.append(scale * pair_sum(two, 2))
        return squeeze(parts)

    own_target = jnp.full((4, 128), tgt[0, 0, 0].astype(F32), F32)
    ES[pl.ds(0, 4), :] = coarsest(lambda m, t: MC[3 + m, t, mid_rows, :], 0.125)
    ES[pl.ds(4, 4), :] = own_target
    EB[2 * NEAR + g] = ES[...]
    for d in (4, 3, 2, 1):
        for sign in (1, -1):
            for core in range(2):
                send(ES, EB.at[2 * (NEAR - sign * d) + g], ebs, ebr, (near_x(sign * d), j, core))
    send(ES, EB.at[2 * NEAR + g], ebs, ebr, (i, j, 1 - g))

    wait(MC.at[pl.ds(0, 6), :, mid_rows, :], mcr)

    @pl.when(i == 0)
    def _():
        MC[pl.ds(0, 3)] = jnp.zeros((3, *MC.shape[1:]), F32)

    @pl.when(i == n_gx - 1)
    def _():
        MC[pl.ds(7, 3)] = jnp.zeros((3, *MC.shape[1:]), F32)

    def mid_first(x, _):
        make_faces(x, MC, mid, 8, 16, 2)
        return 0

    lax.fori_loop(1, 9, mid_first, 0)
    last_face(9, MC, mid, 8, 16)
    wait(MS.at[pl.ds(0, 4), :, mid_rows, :], msr)

    def mid_start(x, _):
        for t in range(2):
            M1[x, t, mid_rows, :] = ME[x, t, mid_rows, :] * (8.0 * MS[x, t, mid_rows, :])
        return 0

    lax.fori_loop(1, 9, mid_start, 0)

    def mid_second(x, _):
        sweep(x, M1, M2, mid, MS, 8.0, 8, 16, 2)
        return 0

    lax.fori_loop(2, 8, mid_second, 0)
    mid_res = [left_over(3 + m, M2, mid, MS, 0.125, 8, 16, 2) for m in range(4)]
    low_src = coarsest(lambda m, t: mid_res[m][t], 0.125)

    GS[...] = low_src
    FS[pl.ds(0, 1), :] = jnp.sum(low_src, axis=0, keepdims=True)
    FS[pl.ds(1, 1), :] = own_target[:1]
    GB[2 * NEAR + g] = low_src
    for d in sorted(range(NEAR + 1, n_gx - NEAR), key=lambda d: -min(d, n_gx - d)):
        for core in range(2):
            send(FS, FB.at[2 * (n_gx - d - NEAR - 1) + g], fs, fr, (near_x(d), j, core))
    for d in (4, 3, 2, 1):
        for sign in (1, -1):
            for core in range(2):
                send(GS, GB.at[2 * (NEAR - sign * d) + g], gs, gr, (near_x(sign * d), j, core))
    send(GS, GB.at[2 * NEAR + g], gs, gr, (i, j, 1 - g))

    for m in range(4):
        for t in range(2):
            SY[m, t] = M2[3 + m, t, pl.ds(12, 8), :]
    send(SY, Y2.at[g], ys, yr, (i, j, 1 - g))
    send(SY, Y2.at[1 - g], ys, yr, (i, near_y(side), 1 - g))
    for m in range(4):
        for t in range(2):
            M2P[3 + m, t, mid_rows, :] = M2[3 + m, t, mid_rows, :]
    wait(Y2, yr)
    for m in range(4):
        for t in range(2):
            M2P[3 + m, t, pl.ds(9, 1), :] = Y2[0, m, t, pl.ds(5, 1), :]
            M2P[3 + m, t, pl.ds(22, 1), :] = Y2[1, m, t, pl.ds(2, 1), :]
    send(M2P.at[pl.ds(4, 3), :, mid_rows, :], M2P.at[pl.ds(0, 3), :, mid_rows, :], xs, xr, (near_x(1), j, g))
    send(M2P.at[pl.ds(3, 3), :, mid_rows, :], M2P.at[pl.ds(7, 3), :, mid_rows, :], xs, xr, (near_x(-1), j, g))

    wait(EB.at[pl.ds(0, 17)], ebr)
    lane = lanes_of(8)
    row = lax.broadcasted_iota(jnp.int32, (8, 128), 0)
    layer, tile, cell = lane // 64, (lane // 32) % 2, lane % 32
    boxes = 2 * NEAR + 1
    zero = jnp.zeros((8, 128), F32)
    coefs, marks = [], []
    for b in range(boxes):
        first, second = EB[2 * b], EB[2 * b + 1]
        coefs.append(jnp.concatenate([first[:4], second[:4]], axis=0))
        marks.append(jnp.where(tile == 0, jnp.broadcast_to(first[4:5], (8, 128)), jnp.broadcast_to(second[4:5], (8, 128))))
    joined = []
    for b in range(boxes - 1):
        touch = lax.rem(i + b - NEAR + n_gx, n_gx) != n_gx - 1
        joined.append(jnp.where((marks[b] == marks[b + 1]) & touch, 1.0, 0.0))

    def along_x(values, ends=None):
        turned = [pltpu.roll(v, 64, 1) for v in values]
        below, above = [], []
        for b in range(boxes):
            before = turned[b - 1] * joined[b - 1] if b else zero
            after = turned[b + 1] * joined[b] if b < boxes - 1 else zero
            below.append(jnp.where(layer == 0, before, turned[b]))
            above.append(jnp.where(layer == 0, turned[b], after))
        return below, above

    def along_yz(v):
        return (pltpu.roll(v, 1, 0), pltpu.roll(v, 7, 0), pltpu.roll(v, 1, 1), pltpu.roll(v, 127, 1))

    keeps = (row > 0, row < 7, cell > 0, cell < 31)
    c_below, c_above = along_x(coefs)
    low_faces, low_ease = [], []
    for b in range(boxes):
        c = coefs[b]
        around = [jnp.where(keep, v, 0.0) for keep, v in zip(keeps, along_yz(c))]
        faces = [c + c_below[b], c + c_above[b]] + [c + v for v in around]
        total = faces[0] + faces[1] + faces[2] + faces[3] + faces[4] + faces[5]
        low_faces.append(faces[:2] + [jnp.where(keep, f, 0.0) for keep, f in zip(keeps, faces[2:])])
        low_ease.append(RELAX / total)

    wait(GB.at[pl.ds(0, 17)], gr)
    wait(FB, fr)
    rhs = [jnp.concatenate([GB[2 * b], GB[2 * b + 1]], axis=0) for b in range(boxes)]
    sums = [jnp.sum(v, axis=0, keepdims=True) for v in rhs]
    names = [m[:1] for m in marks]
    top_tile = tile[:1]
    for d in range(n_gx - boxes):
        first, second = FB[2 * d], FB[2 * d + 1]
        sums.append(first[:1] + second[:1])
        names.append(jnp.where(top_tile == 0, first[1:], second[1:]))
    sums = jnp.concatenate(sums, axis=0)
    names = jnp.concatenate(names, axis=0)
    src_lane = lax.broadcasted_iota(jnp.int32, (128, 128), 0)
    dst_lane = lax.broadcasted_iota(jnp.int32, (128, 128), 1)
    same_tile = jnp.where((src_lane // 32) % 2 == (dst_lane // 32) % 2, 1.0, 0.0).astype(F32)
    sums = exact_dot(sums, same_tile)
    low = []
    for b in range(boxes):
        same = names == names[b:b + 1]
        total = jnp.sum(jnp.where(same, sums, 0.0), axis=0, keepdims=True)
        number = jnp.sum(jnp.where(same, 512.0, 0.0), axis=0, keepdims=True)
        low.append(jnp.broadcast_to(4.0 * total / jnp.maximum(number, 1.0), (8, 128)))

    for number in range(BOTTOM):
        below, above = along_x(low)
        fresh = []
        for b in range(boxes):
            around = [below[b], above[b], *along_yz(low[b])]
            total = 32.0 * rhs[b]
            for face, value in zip(low_faces[b], around):
                total = total + face * value
            fresh.append(0.2 * low[b] + low_ease[b] * total)
        low = fresh

    for b in range(3):
        SQ[b] = low[NEAR - 1 + b]
    send(SQ, Q.at[:, pl.ds(pl.multiple_of(16 - 16 * g, 8), 8), :], qs, qr, (i, near_y(side), 1 - g))
    for b in range(3):
        Q[b, pl.ds(8, 8), :] = low[NEAR - 1 + b]
    wait(M2P.at[pl.ds(0, 6), :, mid_rows, :], xr)
    wait(SQ, qr)
    fix = jnp.concatenate(
        [jnp.where(g == 0, Q[b, pl.ds(6, 8), :], Q[b, pl.ds(10, 8), :]) for b in range(3)], axis=0
    )
    for part in range(4):
        wide = exact_dot(fix, spread_matrix(part))
        for b in range(3):
            PK[2 * b + part // 2, part % 2, pl.ds(0, 8, stride=2), :] = wide[8 * b:8 * b + 8]
            PK[2 * b + part // 2, part % 2, pl.ds(1, 8, stride=2), :] = wide[8 * b:8 * b + 8]

    def corrected(x, _):
        for t in range(2):
            better = M2P[x, t, mid_rows, :] + PK[(x + 1) // 2, t]
            M3[x, t, mid_rows, :] = jnp.where(MC[x, t, mid_rows, :] > 0.0, better, 0.0)
        return 0

    lax.fori_loop(0, 10, corrected, 0)

    def mid_third(x, _):
        sweep(x, M3, M4, mid, MS, 8.0, 8, 16, 2)
        return 0

    lax.fori_loop(1, 9, mid_third, 0)

    def mid_fourth(x, _):
        sweep(x, M4, M1, mid, MS, 8.0, 8, 16, 2)
        for t in range(2):
            PF[pl.ds(0, 16, stride=2), :] = M1[x, t, mid_rows, :]
            PF[pl.ds(1, 16, stride=2), :] = M1[x, t, mid_rows, :]
            for half in range(2):
                V3[2 * x - 2 + half, t, pl.ds(8, 32), :] = V2[2 * x - 2 + half, t, pl.ds(8, 32), :] + PF[...]
        return 0

    lax.fori_loop(2, 8, mid_fourth, 0)

    def fine_third(x, _):
        sweep(x, V3, V1, fine, S, 2.0, 8, 32, 1)
        return 0

    lax.fori_loop(3, 13, fine_third, 0)

    def fine_fourth(x, _):
        at = pl.ds(16, 16)
        sums, own = pull(x, V1, fine, 16, 16, 1)
        for t in range(2):
            FO[x - 4, t] = 0.2 * own[t] + E[x, t, at, :] * (2.0 * S[x, t, at, :] + sums[t])
        return 0

    lax.fori_loop(4, 12, fine_fourth, 0)

    out_rows = pl.ds(pl.multiple_of(16 * g, 8), 16)
    send(FO.at[:, 1 - g], out.at[:, out_rows, :], os_, or_, (i, j, 1 - g))
    keep = pltpu.make_async_copy(FO.at[:, g], out.at[:, out_rows, :], local.at[2])
    keep.start()

    wait(c_bytes, e1s.at[0])
    wait(s_bytes, e1s.at[1])
    wait(MC.at[pl.ds(0, 6), :, mid_rows, :], mcs)
    wait(MS.at[pl.ds(0, 4), :, mid_rows, :], mss)
    wait(EB.at[pl.ds(0, 17)], ebs)
    wait(GB.at[pl.ds(0, 17)], gs)
    wait(FB, fs)
    wait(Y2, ys)
    wait(M2P.at[pl.ds(0, 6), :, mid_rows, :], xs)
    wait(SQ, qs)
    keep.wait()
    wait(FO.at[:, 0], os_)
    wait(out.at[:, pl.ds(0, 16), :], or_)


def solution(mesh):
    n_gx, n_gy = mesh.shape["gx"], mesh.shape["gy"]

    def kernel(*refs):
        cycle(n_gx, n_gy, *refs)

    def per_device(source, beta_cells, target):
        fine = pltpu.VMEM((16, 2, 48, 128), F32)
        mid = pltpu.VMEM((10, 2, 32, 128), F32)
        far = n_gx - 2 * NEAR - 1
        dma = pltpu.SemaphoreType.DMA
        return pl.pallas_call(
            kernel,
            out_shape=jax.ShapeDtypeStruct(source.shape, F32),
            in_specs=[
                pl.BlockSpec(memory_space=pl.ANY),
                pl.BlockSpec(memory_space=pl.ANY),
                pl.BlockSpec(memory_space=pltpu.SMEM),
            ],
            out_specs=pl.BlockSpec(memory_space=pl.ANY),
            scratch_shapes=[
                *[fine] * 11,
                *[mid] * 13,
                pltpu.VMEM((4, 2, 32, 128), F32),
                pltpu.VMEM((4, 2, 32, 128), F32),
                pltpu.VMEM((2, 2, 16, 128), F32),
                pltpu.VMEM((4, 2, 8, 128), F32),
                pltpu.VMEM((2, 4, 2, 8, 128), F32),
                pltpu.VMEM((8, 128), F32),
                pltpu.VMEM((4 * NEAR + 2, 8, 128), F32),
                pltpu.VMEM((8, 128), F32),
                pltpu.VMEM((4 * NEAR + 2, 4, 128), F32),
                pltpu.VMEM((4, 128), F32),
                pltpu.VMEM((2 * far, 2, 128), F32),
                pltpu.VMEM((2, 128), F32),
                pltpu.VMEM((3, 24, 128), F32),
                pltpu.VMEM((3, 8, 128), F32),
                pltpu.VMEM((6, 2, 16, 128), F32),
                pltpu.VMEM((32, 128), F32),
                pltpu.VMEM((8, 2, 16, 128), F32),
                dma((3,)),
                dma((2,)),
                dma((2,)),
                *[dma] * 18,
            ],
            compiler_params=pltpu.CompilerParams(
                collective_id=0, has_side_effects=True, vmem_limit_bytes=32 * 2**20
            ),
            name="cycle",
        )(source, beta_cells, target)

    spec = P("gx", "gy", "gz")
    return jax.shard_map(
        per_device, mesh=mesh, in_specs=(spec, spec, spec), out_specs=spec, check_vma=False
    )
```

time: 341 us -> 52 us (0.15)
  the two profiles are of different devices: /device:TPU:25 before, /device:TPU:1 now
where the time goes in v1:
time: 52 us; the launch traced here: 51.8 us
  Pallas kernels  48.7 us (94%)
  local copies, waits for them, and re-layouts  2.46 us (5%)
  between operations  0.67 us (1%)
    pallas_call x1, Pallas kernels, per_device(): pl.pallas_call(kernel, out_shape=jax.ShapeDtypeStruct(source.shape, F32),...  48.7 us
    unnamed x5, local copies, waits for them, and re-layouts  2.46 us

profile of v1, /device:TPU:1, one launch (start us, length us, event | category | flops | bytes accessed | tf_op | source)
XLA Modules:
  0.0 51.8 jit_solution(585598270333723025)
XLA Ops:
  0.7 0.0 copy-start
  0.7 0.9 %copy-done = f32[8,32,128]{2,1,0:T(8,128)S(1)} copy-done((f32[8,32,128]{2,1,0:T(8,128)S(1)}, f32[8,32,128]{2,1,0:T(8,128)}, u32[]{:S(2)}) %copy-start) | copy-done | bytes 131096
  1.6 0.0 copy-start.1
  1.6 0.9 %copy-done.1 = f32[8,32,128]{2,1,0:T(8,128)S(1)} copy-done((f32[8,32,128]{2,1,0:T(8,128)S(1)}, f32[8,32,128]{2,1,0:T(8,128)}, u32[]{:S(2)}) %copy-start.1) | copy-done | bytes 131096
  2.5 48.7 %cycle.1 = f32[8,32,128]{2,1,0:T(8,128)S(1)} custom-call(f32[8,32,128]{2,1,0:T(8,128)S(1)} %copy-done, f32[8,32,128]{2,1,0:T(8,128)S(1)} %copy-done.1, s32[1,1,1]{2,1,0:T(1,128)S(6)} %copy.5.refs_2_), custom_call_target="tpu_custom_call" | custom-call | tf_op jit(solution)/shard_map/cycle/pallas_call | solution.py:492
  51.1 0.7 %copy.6 = f32[8,32,128]{2,1,0:T(8,128)} copy(f32[8,32,128]{2,1,0:T(8,128)S(1)} %cycle.1) | data formatting | bytes 262144
Async XLA Ops:
  0.7 0.9 %copy-start = (f32[8,32,128]{2,1,0:T(8,128)S(1)}, f32[8,32,128]{2,1,0:T(8,128)}, u32[]{:S(2)}) copy-start(f32[8,32,128]{2,1,0:T(8,128)} %refs_0_.1) | copy-start | bytes 393220
  1.6 0.9 %copy-start.1 = (f32[8,32,128]{2,1,0:T(8,128)S(1)}, f32[8,32,128]{2,1,0:T(8,128)}, u32[]{:S(2)}) copy-start(f32[8,32,128]{2,1,0:T(8,128)} %refs_1_.1) | copy-start | bytes 393220

commit v2 on v1

--- a/solution.py
+++ b/solution.py
@@ -118,7 +118,7 @@
     (C, S, FX, FY, FL, FR, W, E, V1, V2, V3,
      MC, MS, MFX, MFY, MFL, MFR, MW, ME, M1, M2, M2P, M3, M4,
      RS, RC, R2, SY, Y2, SX, EB, ES, GB, GS, FB, FS, Q, SQ, PK, PF, FO,
-     local, e1s, e1r, mcs, mcr, mss, msr, ebs, ebr, gs, gr, fs, fr, ys, yr, xs, xr, qs, qr, os_, or_) = scratch
+     local, e1s, e1r, mcs, mcr, mss, msr, ebs, ebr, gs, gr, fs, fr, ys, yr, xs, xr, qs, qr, os_, or_, known) = scratch
     i, j, g = lax.axis_index("gx"), lax.axis_index("gy"), lax.axis_index("gz")
     fine = (FX, FY, FL, FR, W, E)
     mid = (MFX, MFY, MFL, MFR, MW, ME)
@@ -135,6 +135,10 @@
             device_id=where, device_id_type=MESH,
         ).start()
 
+    def tell(step):
+        for sign in (1, -1):
+            pl.semaphore_signal(known.at[step], inc=1, device_id=(near_x(sign * 3), j, g), device_id_type=MESH)
+
     def wait(ref, sem):
         pltpu.make_async_copy(ref, ref, sem).wait()
 
@@ -145,17 +149,20 @@
 
     barrier = pltpu.get_barrier_semaphore()
     side = 2 * g - 1
-    count = 0
-    for d in range(1, n_gx):
-        for core in range(2):
-            pl.semaphore_signal(barrier, inc=1, device_id=(near_x(d), j, core), device_id_type=MESH)
-            count += 1
+
+    def greet(where):
+        pl.semaphore_signal(barrier, inc=1, device_id=where, device_id_type=MESH)
+
     for dx in (-1, 0, 1):
         for core in range(2):
-            pl.semaphore_signal(barrier, inc=1, device_id=(near_x(dx), near_y(side), core), device_id_type=MESH)
-            count += 1
-    pl.semaphore_signal(barrier, inc=1, device_id=(i, j, 1 - g), device_id_type=MESH)
-    pl.semaphore_wait(barrier, count + 1)
+            greet((near_x(dx), near_y(side), core))
+    for dx in (3, 2, 1):
+        for sign in (1, -1):
+            for core in range(2 if dx < 3 else 1):
+                greet((near_x(sign * dx), j, core if dx < 3 else g))
+    greet((i, j, 1 - g))
+    pl.semaphore_wait(barrier, 17)
+    tell(0)
 
     for index, (field, target, deep) in enumerate(((beta, C, 4), (src, S, 3))):
         ss, rs = e1s.at[index], e1r.at[index]
@@ -209,6 +216,9 @@
     send(MC.at[pl.ds(4, 3), :, mid_rows, :], MC.at[pl.ds(0, 3), :, mid_rows, :], mcs, mcr, (near_x(1), j, g))
     send(MC.at[pl.ds(3, 3), :, mid_rows, :], MC.at[pl.ds(7, 3), :, mid_rows, :], mcs, mcr, (near_x(-1), j, g))
 
+    pl.semaphore_wait(known.at[0], 2)
+    tell(1)
+
     wait(src.at[:, pl.ds(0, 24), :], local.at[1])
     wait(s_bytes, e1r.at[1])
 
@@ -299,6 +309,7 @@
     mid_res = [left_over(3 + m, M2, mid, MS, 0.125, 8, 16, 2) for m in range(4)]
     low_src = coarsest(lambda m, t: mid_res[m][t], 0.125)
 
+    pl.semaphore_wait(known.at[1], 2)
     GS[...] = low_src
     FS[pl.ds(0, 1), :] = jnp.sum(low_src, axis=0, keepdims=True)
     FS[pl.ds(1, 1), :] = own_target[:1]
@@ -493,8 +504,8 @@
             kernel,
             out_shape=jax.ShapeDtypeStruct(source.shape, F32),
             in_specs=[
-                pl.BlockSpec(memory_space=pl.ANY),
-                pl.BlockSpec(memory_space=pl.ANY),
+                pl.BlockSpec(memory_space=pltpu.HBM),
+                pl.BlockSpec(memory_space=pltpu.HBM),
                 pl.BlockSpec(memory_space=pltpu.SMEM),
             ],
             out_specs=pl.BlockSpec(memory_space=pl.ANY),
@@ -522,6 +533,7 @@
                 dma((2,)),
                 dma((2,)),
                 *[dma] * 18,
+                pltpu.SemaphoreType.REGULAR((2,)),
             ],
             compiler_params=pltpu.CompilerParams(
                 collective_id=0, has_side_effects=True, vmem_limit_bytes=32 * 2**20

time: 52 us -> 50.7 us (0.975)
  Pallas kernels: 48.7 us -> 47.4 us
    pallas_call x1, Pallas kernels: 48.7 us -> 47.4 us  [per_device(): pl.pallas_call(kernel, out_shape=jax.ShapeDtypeStruct(source.shape, F32),...]
where the time goes in v2:
time: 50.7 us; the launch traced here: 50.5 us
  Pallas kernels  47.4 us (93%)
  local copies, waits for them, and re-layouts  2.46 us (5%)
  between operations  0.67 us (1%)
    pallas_call x1, Pallas kernels, per_device(): pl.pallas_call(kernel, out_shape=jax.ShapeDtypeStruct(source.shape, F32),...  47.4 us
    unnamed x5, local copies, waits for them, and re-layouts  2.46 us

profile of v2, /device:TPU:1, one launch (start us, length us, event | category | flops | bytes accessed | tf_op | source)
XLA Modules:
  0.0 50.5 jit_solution(4754855920683293899)
XLA Ops:
  0.7 0.0 copy-start
  0.7 0.9 %copy-done = f32[8,32,128]{2,1,0:T(8,128)S(1)} copy-done((f32[8,32,128]{2,1,0:T(8,128)S(1)}, f32[8,32,128]{2,1,0:T(8,128)}, u32[]{:S(2)}) %copy-start) | copy-done | bytes 131096
  1.6 0.0 copy-start.1
  1.6 0.9 %copy-done.1 = f32[8,32,128]{2,1,0:T(8,128)S(1)} copy-done((f32[8,32,128]{2,1,0:T(8,128)S(1)}, f32[8,32,128]{2,1,0:T(8,128)}, u32[]{:S(2)}) %copy-start.1) | copy-done | bytes 131096
  2.5 47.4 %cycle.1 = f32[8,32,128]{2,1,0:T(8,128)S(1)} custom-call(f32[8,32,128]{2,1,0:T(8,128)S(1)} %copy-done, f32[8,32,128]{2,1,0:T(8,128)S(1)} %copy-done.1, s32[1,1,1]{2,1,0:T(1,128)S(6)} %copy.5.refs_2_), custom_call_target="tpu_custom_call" | custom-call | tf_op jit(solution)/shard_map/cycle/pallas_call | solution.py:503
  49.9 0.7 %copy.6 = f32[8,32,128]{2,1,0:T(8,128)} copy(f32[8,32,128]{2,1,0:T(8,128)S(1)} %cycle.1) | data formatting | bytes 262144
Async XLA Ops:
  0.7 0.9 %copy-start = (f32[8,32,128]{2,1,0:T(8,128)S(1)}, f32[8,32,128]{2,1,0:T(8,128)}, u32[]{:S(2)}) copy-start(f32[8,32,128]{2,1,0:T(8,128)} %refs_0_.1) | copy-start | bytes 393220
  1.6 0.9 %copy-start.1 = (f32[8,32,128]{2,1,0:T(8,128)S(1)}, f32[8,32,128]{2,1,0:T(8,128)}, u32[]{:S(2)}) copy-start(f32[8,32,128]{2,1,0:T(8,128)} %refs_1_.1) | copy-start | bytes 393220

commit v3 on v2

--- a/solution.py
+++ b/solution.py
@@ -11,6 +11,11 @@
 F32 = jnp.float32
 MESH = pl.DeviceIdType.MESH
 NEAR = 4
+
+
+def layers(low, high, work):
+    for x in range(low, high):
+        work(x, 0)
 
 
 def lanes_of(rows):
@@ -102,23 +107,27 @@
     return jnp.dot(a, b, precision=lax.Precision.HIGHEST, preferred_element_type=F32)
 
 
-def squeeze_matrix(part):
-    src = lax.broadcasted_iota(jnp.int32, (128, 128), 0)
-    dst = lax.broadcasted_iota(jnp.int32, (128, 128), 1)
-    return jnp.where((src == 4 * (dst % 32)) & (dst // 32 == part), 1.0, 0.0).astype(F32)
-
-
-def spread_matrix(part):
-    src = lax.broadcasted_iota(jnp.int32, (128, 128), 0)
-    dst = lax.broadcasted_iota(jnp.int32, (128, 128), 1)
-    return jnp.where(src == 32 * part + dst // 4, 1.0, 0.0).astype(F32)
+def braid(parts):
+    kind = lanes_of(parts[0].shape[0]) % 4
+    return jnp.where(kind < 2, jnp.where(kind == 0, parts[0], parts[1]), jnp.where(kind == 2, parts[2], parts[3]))
+
+
+def unbraid(value):
+    lane = lanes_of(value.shape[0])
+    even, upper = lane % 2 == 0, lane % 4 >= 2
+    pairs = (jnp.where(even, value, pltpu.roll(value, 1, 1)), jnp.where(even, pltpu.roll(value, 127, 1), value))
+    return [
+        jnp.where(upper, pltpu.roll(pair, 2, 1), pair) if half == 0 else jnp.where(upper, pair, pltpu.roll(pair, 126, 1))
+        for half in range(2)
+        for pair in pairs
+    ]
 
 
 def cycle(n_gx, n_gy, src, beta, tgt, out, *scratch):
     (C, S, FX, FY, FL, FR, W, E, V1, V2, V3,
      MC, MS, MFX, MFY, MFL, MFR, MW, ME, M1, M2, M2P, M3, M4,
      RS, RC, R2, SY, Y2, SX, EB, ES, GB, GS, FB, FS, Q, SQ, PK, PF, FO,
-     local, e1s, e1r, mcs, mcr, mss, msr, ebs, ebr, gs, gr, fs, fr, ys, yr, xs, xr, qs, qr, os_, or_, known) = scratch
+     local, e1s, e1r, mcs, mcr, mss, msr, ebs, ebr, gs, gr, fs, fr, ys, yr, xs, xr, qs, qr, os_, or_, vs, vr, known) = scratch
     i, j, g = lax.axis_index("gx"), lax.axis_index("gy"), lax.axis_index("gz")
     fine = (FX, FY, FL, FR, W, E)
     mid = (MFX, MFY, MFL, MFR, MW, ME)
@@ -164,54 +173,47 @@
     pl.semaphore_wait(barrier, 17)
     tell(0)
 
-    for index, (field, target, deep) in enumerate(((beta, C, 4), (src, S, 3))):
-        ss, rs = e1s.at[index], e1r.at[index]
+    for index, (field, target, deep) in enumerate(((beta, C, 3), (src, S, 2))):
+        ss, rs = e1s.at[index], e1r.at[2 * index + 1]
         for dx in (1, -1):
             part = pl.ds(8 - deep, deep) if dx == 1 else pl.ds(0, deep)
             place = pl.ds(4 - deep, deep) if dx == 1 else pl.ds(12, deep)
             for core in range(2):
-                dy = 1 if core == 0 else -1
                 send(field.at[part, pl.ds(24 if core == 0 else 0, 8), :],
                      target.at[place, g, pl.ds(8 if core == 0 else 32, 8), :], ss, rs,
-                     (near_x(dx), near_y(dy), core))
+                     (near_x(dx), near_y(1 if core == 0 else -1), core))
                 send(field.at[part, pl.ds(8 * core, 24), :],
                      target.at[place, g, pl.ds(16 - 8 * core, 24), :], ss, rs, (near_x(dx), j, core))
+    for index, (field, target) in enumerate(((beta, C), (src, S))):
+        ss, rs = e1s.at[index], e1r.at[2 * index]
         for core in range(2):
-            dy = 1 if core == 0 else -1
             send(field.at[:, pl.ds(24 if core == 0 else 0, 8), :],
-                 target.at[pl.ds(4, 8), g, pl.ds(8 if core == 0 else 32, 8), :], ss, rs, (i, near_y(dy), core))
+                 target.at[pl.ds(4, 8), g, pl.ds(8 if core == 0 else 32, 8), :], ss, rs,
+                 (i, near_y(1 if core == 0 else -1), core))
         send(field.at[:, pl.ds(pl.multiple_of(8 - 8 * g, 8), 24), :],
              target.at[pl.ds(4, 8), g, pl.ds(pl.multiple_of(8 + 8 * g, 8), 24), :], ss, rs, (i, j, 1 - g))
 
-    c_bytes = C.at[pl.ds(0, 13), :, pl.ds(0, 32), :]
-    s_bytes = S.at[pl.ds(0, 11), :, pl.ds(0, 32), :]
+    def cells(count):
+        return C.at[pl.ds(0, count), :, pl.ds(0, 32), :]
+
     wait(beta.at[:, pl.ds(0, 24), :], local.at[0])
-    wait(c_bytes, e1r.at[0])
-
-    @pl.when(i == 0)
-    def _():
-        C[pl.ds(0, 4)] = jnp.zeros((4, *C.shape[1:]), F32)
-
-    @pl.when(i == n_gx - 1)
-    def _():
-        C[pl.ds(12, 4)] = jnp.zeros((4, *C.shape[1:]), F32)
+    wait(cells(5), e1r.at[0])
 
     @pl.when((j == 0) & (g == 0))
     def _():
-        C[:, :, pl.ds(8, 8), :] = jnp.zeros((16, 2, 8, 128), F32)
+        C[pl.ds(4, 8), :, pl.ds(8, 8), :] = jnp.zeros((8, 2, 8, 128), F32)
 
     @pl.when((j == n_gy - 1) & (g == 1))
     def _():
-        C[:, :, pl.ds(32, 8), :] = jnp.zeros((16, 2, 8, 128), F32)
+        C[pl.ds(4, 8), :, pl.ds(32, 8), :] = jnp.zeros((8, 2, 8, 128), F32)
 
     def mid_coefficient(m, _):
         for t in range(2):
             RC[m, t] = C[4 + 2 * m, t, pl.ds(8, 32), :] + C[5 + 2 * m, t, pl.ds(8, 32), :]
             two = RC[m, t, pl.ds(0, 16, stride=2), :] + RC[m, t, pl.ds(1, 16, stride=2), :]
             MC[m + 3, t, pl.ds(8, 16), :] = 0.125 * pair_sum(two, 1)
-        return 0
-
-    lax.fori_loop(0, 4, mid_coefficient, 0)
+
+    layers(0, 4, mid_coefficient)
     mid_rows = pl.ds(8, 16)
     send(MC.at[pl.ds(4, 3), :, mid_rows, :], MC.at[pl.ds(0, 3), :, mid_rows, :], mcs, mcr, (near_x(1), j, g))
     send(MC.at[pl.ds(3, 3), :, mid_rows, :], MC.at[pl.ds(7, 3), :, mid_rows, :], mcs, mcr, (near_x(-1), j, g))
@@ -220,22 +222,46 @@
     tell(1)
 
     wait(src.at[:, pl.ds(0, 24), :], local.at[1])
-    wait(s_bytes, e1r.at[1])
+    wait(cells(5), e1r.at[2])
 
     def fine_first(x, _):
         make_faces(x, C, fine, 8, 32, 1)
         for t in range(2):
             V1[x, t, pl.ds(8, 32), :] = E[x, t, pl.ds(8, 32), :] * (2.0 * S[x, t, pl.ds(8, 32), :])
-        return 0
-
-    lax.fori_loop(1, 15, fine_first, 0)
-    last_face(15, C, fine, 8, 32)
 
     def fine_second(x, _):
         sweep(x, V1, V2, fine, S, 2.0, 8, 32, 1)
-        return 0
-
-    lax.fori_loop(2, 14, fine_second, 0)
+
+    layers(5, 11, fine_first)
+    layers(6, 10, fine_second)
+
+    wait(cells(6), e1r.at[1])
+
+    @pl.when(i == 0)
+    def _():
+        C[pl.ds(1, 3)] = jnp.zeros((3, *C.shape[1:]), F32)
+
+    @pl.when(i == n_gx - 1)
+    def _():
+        C[pl.ds(12, 3)] = jnp.zeros((3, *C.shape[1:]), F32)
+
+    @pl.when((j == 0) & (g == 0))
+    def _():
+        for low in (1, 12):
+            C[pl.ds(low, 3), :, pl.ds(8, 8), :] = jnp.zeros((3, 2, 8, 128), F32)
+
+    @pl.when((j == n_gy - 1) & (g == 1))
+    def _():
+        for low in (1, 12):
+            C[pl.ds(low, 3), :, pl.ds(32, 8), :] = jnp.zeros((3, 2, 8, 128), F32)
+
+    wait(cells(4), e1r.at[3])
+    layers(2, 5, fine_first)
+    layers(11, 14, fine_first)
+    last_face(14, C, fine, 8, 32)
+    layers(3, 6, fine_second)
+    layers(10, 13, fine_second)
+    fine_rows = pl.ds(8, 32)
 
     def fine_residual(m, _):
         lower = left_over(4 + 2 * m, V2, fine, S, 0.5, 8, 32, 1)
@@ -244,18 +270,13 @@
             RS[m, t] = lower[t] + upper[t]
             two = RS[m, t, pl.ds(0, 16, stride=2), :] + RS[m, t, pl.ds(1, 16, stride=2), :]
             MS[m + 3, t, mid_rows, :] = 0.125 * pair_sum(two, 1)
-        return 0
-
-    lax.fori_loop(0, 4, fine_residual, 0)
+
+    layers(0, 4, fine_residual)
     send(MS.at[pl.ds(5, 2), :, mid_rows, :], MS.at[pl.ds(1, 2), :, mid_rows, :], mss, msr, (near_x(1), j, g))
     send(MS.at[pl.ds(3, 2), :, mid_rows, :], MS.at[pl.ds(7, 2), :, mid_rows, :], mss, msr, (near_x(-1), j, g))
 
-    def squeeze(parts):
-        total = None
-        for part, value in enumerate(parts):
-            term = exact_dot(value, squeeze_matrix(part))
-            total = term if total is None else total + term
-        return total
+    send(V2.at[10, :, fine_rows, :], V2.at[2, :, fine_rows, :], vs, vr.at[0], (near_x(1), j, g))
+    send(V2.at[5, :, fine_rows, :], V2.at[13, :, fine_rows, :], vs, vr.at[1], (near_x(-1), j, g))
 
     def coarsest(field, scale):
         parts = []
@@ -264,7 +285,7 @@
                 R2[layer, t] = field(2 * layer, t) + field(2 * layer + 1, t)
                 two = R2[layer, t, pl.ds(4, 4, stride=2), :] + R2[layer, t, pl.ds(5, 4, stride=2), :]
                 parts.append(scale * pair_sum(two, 2))
-        return squeeze(parts)
+        return braid(parts)
 
     own_target = jnp.full((4, 128), tgt[0, 0, 0].astype(F32), F32)
     ES[pl.ds(0, 4), :] = coarsest(lambda m, t: MC[3 + m, t, mid_rows, :], 0.125)
@@ -288,24 +309,21 @@
 
     def mid_first(x, _):
         make_faces(x, MC, mid, 8, 16, 2)
-        return 0
-
-    lax.fori_loop(1, 9, mid_first, 0)
+
+    layers(1, 9, mid_first)
     last_face(9, MC, mid, 8, 16)
     wait(MS.at[pl.ds(0, 4), :, mid_rows, :], msr)
 
     def mid_start(x, _):
         for t in range(2):
             M1[x, t, mid_rows, :] = ME[x, t, mid_rows, :] * (8.0 * MS[x, t, mid_rows, :])
-        return 0
-
-    lax.fori_loop(1, 9, mid_start, 0)
+
+    layers(1, 9, mid_start)
 
     def mid_second(x, _):
         sweep(x, M1, M2, mid, MS, 8.0, 8, 16, 2)
-        return 0
-
-    lax.fori_loop(2, 8, mid_second, 0)
+
+    layers(2, 8, mid_second)
     mid_res = [left_over(3 + m, M2, mid, MS, 0.125, 8, 16, 2) for m in range(4)]
     low_src = coarsest(lambda m, t: mid_res[m][t], 0.125)
 
@@ -342,7 +360,7 @@
     wait(EB.at[pl.ds(0, 17)], ebr)
     lane = lanes_of(8)
     row = lax.broadcasted_iota(jnp.int32, (8, 128), 0)
-    layer, tile, cell = lane // 64, (lane // 32) % 2, lane % 32
+    layer, tile, cell = (lane % 4) // 2, lane % 2, lane // 4
     boxes = 2 * NEAR + 1
     zero = jnp.zeros((8, 128), F32)
     coefs, marks = [], []
@@ -355,18 +373,19 @@
         touch = lax.rem(i + b - NEAR + n_gx, n_gx) != n_gx - 1
         joined.append(jnp.where((marks[b] == marks[b + 1]) & touch, 1.0, 0.0))
 
-    def along_x(values, ends=None):
-        turned = [pltpu.roll(v, 64, 1) for v in values]
+    def along_x(values):
+        down = [pltpu.roll(v, 2, 1) for v in values]
+        up = [pltpu.roll(v, 126, 1) for v in values]
         below, above = [], []
         for b in range(boxes):
-            before = turned[b - 1] * joined[b - 1] if b else zero
-            after = turned[b + 1] * joined[b] if b < boxes - 1 else zero
-            below.append(jnp.where(layer == 0, before, turned[b]))
-            above.append(jnp.where(layer == 0, turned[b], after))
+            before = up[b - 1] * joined[b - 1] if b else zero
+            after = down[b + 1] * joined[b] if b < boxes - 1 else zero
+            below.append(jnp.where(layer == 0, before, down[b]))
+            above.append(jnp.where(layer == 0, up[b], after))
         return below, above
 
     def along_yz(v):
-        return (pltpu.roll(v, 1, 0), pltpu.roll(v, 7, 0), pltpu.roll(v, 1, 1), pltpu.roll(v, 127, 1))
+        return (pltpu.roll(v, 1, 0), pltpu.roll(v, 7, 0), pltpu.roll(v, 4, 1), pltpu.roll(v, 124, 1))
 
     keeps = (row > 0, row < 7, cell > 0, cell < 31)
     c_below, c_above = along_x(coefs)
@@ -379,103 +398,105 @@
         low_faces.append(faces[:2] + [jnp.where(keep, f, 0.0) for keep, f in zip(keeps, faces[2:])])
         low_ease.append(RELAX / total)
 
+    def solve(low, rhs):
+        for number in range(BOTTOM):
+            below, above = along_x(low)
+            fresh = []
+            for b in range(boxes):
+                around = [below[b], above[b], *along_yz(low[b])]
+                total = low_faces[b][0] * around[0]
+                for face, value in zip(low_faces[b][1:], around[1:]):
+                    total = total + face * value
+                if rhs is not None:
+                    total = total + 32.0 * rhs[b]
+                fresh.append(0.2 * low[b] + low_ease[b] * total)
+            low = fresh
+        return low[NEAR - 1:NEAR + 2]
+
+    from_mean = solve([jnp.full((8, 128), 4.0, F32)] * boxes, None)
     wait(GB.at[pl.ds(0, 17)], gr)
-    wait(FB, fr)
     rhs = [jnp.concatenate([GB[2 * b], GB[2 * b + 1]], axis=0) for b in range(boxes)]
+    from_source = solve([zero] * boxes, rhs)
     sums = [jnp.sum(v, axis=0, keepdims=True) for v in rhs]
     names = [m[:1] for m in marks]
     top_tile = tile[:1]
+    src_lane = lax.broadcasted_iota(jnp.int32, (128, 128), 0)
+    dst_lane = lax.broadcasted_iota(jnp.int32, (128, 128), 1)
+    same_tile = jnp.where(src_lane % 2 == dst_lane % 2, 1.0, 0.0).astype(F32)
+
+    wait(FB, fr)
     for d in range(n_gx - boxes):
         first, second = FB[2 * d], FB[2 * d + 1]
         sums.append(first[:1] + second[:1])
         names.append(jnp.where(top_tile == 0, first[1:], second[1:]))
-    sums = jnp.concatenate(sums, axis=0)
+    sums = exact_dot(jnp.concatenate(sums, axis=0), same_tile)
     names = jnp.concatenate(names, axis=0)
-    src_lane = lax.broadcasted_iota(jnp.int32, (128, 128), 0)
-    dst_lane = lax.broadcasted_iota(jnp.int32, (128, 128), 1)
-    same_tile = jnp.where((src_lane // 32) % 2 == (dst_lane // 32) % 2, 1.0, 0.0).astype(F32)
-    sums = exact_dot(sums, same_tile)
     low = []
-    for b in range(boxes):
-        same = names == names[b:b + 1]
+    for b in range(3):
+        here = NEAR - 1 + b
+        same = names == names[here:here + 1]
         total = jnp.sum(jnp.where(same, sums, 0.0), axis=0, keepdims=True)
         number = jnp.sum(jnp.where(same, 512.0, 0.0), axis=0, keepdims=True)
-        low.append(jnp.broadcast_to(4.0 * total / jnp.maximum(number, 1.0), (8, 128)))
-
-    for number in range(BOTTOM):
-        below, above = along_x(low)
-        fresh = []
-        for b in range(boxes):
-            around = [below[b], above[b], *along_yz(low[b])]
-            total = 32.0 * rhs[b]
-            for face, value in zip(low_faces[b], around):
-                total = total + face * value
-            fresh.append(0.2 * low[b] + low_ease[b] * total)
-        low = fresh
+        low.append(from_source[b] + (total / jnp.maximum(number, 1.0)) * from_mean[b])
 
     for b in range(3):
-        SQ[b] = low[NEAR - 1 + b]
+        SQ[b] = low[b]
     send(SQ, Q.at[:, pl.ds(pl.multiple_of(16 - 16 * g, 8), 8), :], qs, qr, (i, near_y(side), 1 - g))
     for b in range(3):
-        Q[b, pl.ds(8, 8), :] = low[NEAR - 1 + b]
+        Q[b, pl.ds(8, 8), :] = low[b]
     wait(M2P.at[pl.ds(0, 6), :, mid_rows, :], xr)
     wait(SQ, qr)
-    fix = jnp.concatenate(
-        [jnp.where(g == 0, Q[b, pl.ds(6, 8), :], Q[b, pl.ds(10, 8), :]) for b in range(3)], axis=0
-    )
-    for part in range(4):
-        wide = exact_dot(fix, spread_matrix(part))
-        for b in range(3):
-            PK[2 * b + part // 2, part % 2, pl.ds(0, 8, stride=2), :] = wide[8 * b:8 * b + 8]
-            PK[2 * b + part // 2, part % 2, pl.ds(1, 8, stride=2), :] = wide[8 * b:8 * b + 8]
+    for b in range(3):
+        fix = jnp.where(g == 0, Q[b, pl.ds(6, 8), :], Q[b, pl.ds(10, 8), :])
+        for part, wide in enumerate(unbraid(fix)):
+            PK[2 * b + part // 2, part % 2, pl.ds(0, 8, stride=2), :] = wide
+            PK[2 * b + part // 2, part % 2, pl.ds(1, 8, stride=2), :] = wide
 
     def corrected(x, _):
         for t in range(2):
             better = M2P[x, t, mid_rows, :] + PK[(x + 1) // 2, t]
             M3[x, t, mid_rows, :] = jnp.where(MC[x, t, mid_rows, :] > 0.0, better, 0.0)
-        return 0
-
-    lax.fori_loop(0, 10, corrected, 0)
+
+    layers(0, 10, corrected)
 
     def mid_third(x, _):
         sweep(x, M3, M4, mid, MS, 8.0, 8, 16, 2)
-        return 0
-
-    lax.fori_loop(1, 9, mid_third, 0)
+
+    layers(1, 9, mid_third)
+    wait(V2.at[0, :, fine_rows, :], vr.at[0])
+    wait(V2.at[0, :, fine_rows, :], vr.at[1])
 
     def mid_fourth(x, _):
         sweep(x, M4, M1, mid, MS, 8.0, 8, 16, 2)
         for t in range(2):
-            PF[pl.ds(0, 16, stride=2), :] = M1[x, t, mid_rows, :]
-            PF[pl.ds(1, 16, stride=2), :] = M1[x, t, mid_rows, :]
+            PF[x - 2, t, pl.ds(0, 16, stride=2), :] = M1[x, t, mid_rows, :]
+            PF[x - 2, t, pl.ds(1, 16, stride=2), :] = M1[x, t, mid_rows, :]
             for half in range(2):
-                V3[2 * x - 2 + half, t, pl.ds(8, 32), :] = V2[2 * x - 2 + half, t, pl.ds(8, 32), :] + PF[...]
-        return 0
-
-    lax.fori_loop(2, 8, mid_fourth, 0)
+                V3[2 * x - 2 + half, t, fine_rows, :] = V2[2 * x - 2 + half, t, fine_rows, :] + PF[x - 2, t]
+
+    layers(2, 8, mid_fourth)
 
     def fine_third(x, _):
-        sweep(x, V3, V1, fine, S, 2.0, 8, 32, 1)
-        return 0
-
-    lax.fori_loop(3, 13, fine_third, 0)
+        sweep(x, V3, V1, fine, S, 2.0, 15, 18, 1)
+
+    layers(3, 13, fine_third)
 
     def fine_fourth(x, _):
         at = pl.ds(16, 16)
         sums, own = pull(x, V1, fine, 16, 16, 1)
         for t in range(2):
             FO[x - 4, t] = 0.2 * own[t] + E[x, t, at, :] * (2.0 * S[x, t, at, :] + sums[t])
-        return 0
-
-    lax.fori_loop(4, 12, fine_fourth, 0)
+
+    layers(4, 12, fine_fourth)
 
     out_rows = pl.ds(pl.multiple_of(16 * g, 8), 16)
     send(FO.at[:, 1 - g], out.at[:, out_rows, :], os_, or_, (i, j, 1 - g))
     keep = pltpu.make_async_copy(FO.at[:, g], out.at[:, out_rows, :], local.at[2])
     keep.start()
 
-    wait(c_bytes, e1s.at[0])
-    wait(s_bytes, e1s.at[1])
+    wait(cells(11), e1s.at[0])
+    wait(cells(9), e1s.at[1])
+    wait(V2.at[pl.ds(0, 2), :, fine_rows, :], vs)
     wait(MC.at[pl.ds(0, 6), :, mid_rows, :], mcs)
     wait(MS.at[pl.ds(0, 4), :, mid_rows, :], mss)
     wait(EB.at[pl.ds(0, 17)], ebs)
@@ -527,12 +548,13 @@
                 pltpu.VMEM((3, 24, 128), F32),
                 pltpu.VMEM((3, 8, 128), F32),
                 pltpu.VMEM((6, 2, 16, 128), F32),
-                pltpu.VMEM((32, 128), F32),
+                pltpu.VMEM((6, 2, 32, 128), F32),
                 pltpu.VMEM((8, 2, 16, 128), F32),
                 dma((3,)),
                 dma((2,)),
+                dma((4,)),
+                *[dma] * 19,
                 dma((2,)),
-                *[dma] * 18,
                 pltpu.SemaphoreType.REGULAR((2,)),
             ],
             compiler_params=pltpu.CompilerParams(

time: 50.7 us -> 43 us (0.85)
  Pallas kernels: 47.4 us -> 39.7 us
    pallas_call x1, Pallas kernels: 47.4 us -> 39.7 us  [per_device(): pl.pallas_call(kernel, out_shape=jax.ShapeDtypeStruct(source.shape, F32),...]
where the time goes in v3:
time: 43 us; the launch traced here: 42.8 us
  Pallas kernels  39.7 us (92%)
  local copies, waits for them, and re-layouts  2.46 us (6%)
  between operations  0.67 us (2%)
    pallas_call x1, Pallas kernels, per_device(): pl.pallas_call(kernel, out_shape=jax.ShapeDtypeStruct(source.shape, F32),...  39.7 us
    unnamed x5, local copies, waits for them, and re-layouts  2.46 us

profile of v3, /device:TPU:1, one launch (start us, length us, event | category | flops | bytes accessed | tf_op | source)
XLA Modules:
  0.0 42.8 jit_solution(3201406317578668721)
XLA Ops:
  0.7 0.0 copy-start
  0.7 0.9 %copy-done = f32[8,32,128]{2,1,0:T(8,128)S(1)} copy-done((f32[8,32,128]{2,1,0:T(8,128)S(1)}, f32[8,32,128]{2,1,0:T(8,128)}, u32[]{:S(2)}) %copy-start) | copy-done | bytes 131096
  1.6 0.0 copy-start.1
  1.6 0.9 %copy-done.1 = f32[8,32,128]{2,1,0:T(8,128)S(1)} copy-done((f32[8,32,128]{2,1,0:T(8,128)S(1)}, f32[8,32,128]{2,1,0:T(8,128)}, u32[]{:S(2)}) %copy-start.1) | copy-done | bytes 131096
  2.5 39.7 %cycle.1 = f32[8,32,128]{2,1,0:T(8,128)S(1)} custom-call(f32[8,32,128]{2,1,0:T(8,128)S(1)} %copy-done, f32[8,32,128]{2,1,0:T(8,128)S(1)} %copy-done.1, s32[1,1,1]{2,1,0:T(1,128)S(6)} %copy.5.refs_2_), custom_call_target="tpu_custom_call" | custom-call | tf_op jit(solution)/shard_map/cycle/pallas_call | solution.py:524
  42.2 0.7 %copy.6 = f32[8,32,128]{2,1,0:T(8,128)} copy(f32[8,32,128]{2,1,0:T(8,128)S(1)} %cycle.1) | data formatting | bytes 262144
Async XLA Ops:
  0.7 0.9 %copy-start = (f32[8,32,128]{2,1,0:T(8,128)S(1)}, f32[8,32,128]{2,1,0:T(8,128)}, u32[]{:S(2)}) copy-start(f32[8,32,128]{2,1,0:T(8,128)} %refs_0_.1) | copy-start | bytes 393220
  1.6 0.9 %copy-start.1 = (f32[8,32,128]{2,1,0:T(8,128)S(1)}, f32[8,32,128]{2,1,0:T(8,128)}, u32[]{:S(2)}) copy-start(f32[8,32,128]{2,1,0:T(8,128)} %refs_1_.1) | copy-start | bytes 393220

commit v4 on v3

--- a/solution.py
+++ b/solution.py
@@ -158,54 +158,71 @@
 
     barrier = pltpu.get_barrier_semaphore()
     side = 2 * g - 1
+    up, down = j < n_gy - 1, j > 0
+    has_side = jnp.where(g == 0, j, n_gy - 1 - j) > 0
 
     def greet(where):
         pl.semaphore_signal(barrier, inc=1, device_id=where, device_id_type=MESH)
 
-    for dx in (-1, 0, 1):
-        for core in range(2):
-            greet((near_x(dx), near_y(side), core))
+    @pl.when(has_side)
+    def _():
+        for dx in (-1, 0, 1):
+            for core in range(2):
+                greet((near_x(dx), near_y(side), core))
+
     for dx in (3, 2, 1):
         for sign in (1, -1):
             for core in range(2 if dx < 3 else 1):
                 greet((near_x(sign * dx), j, core if dx < 3 else g))
     greet((i, j, 1 - g))
-    pl.semaphore_wait(barrier, 17)
+    pl.semaphore_wait(barrier, 11 + 3 * (up.astype(jnp.int32) + down.astype(jnp.int32)))
     tell(0)
 
-    for index, (field, target, deep) in enumerate(((beta, C, 3), (src, S, 2))):
-        ss, rs = e1s.at[index], e1r.at[2 * index + 1]
+    fields = ((beta, C, 3), (src, S, 2))
+    for index, (field, target, deep) in enumerate(fields):
         for dx in (1, -1):
             part = pl.ds(8 - deep, deep) if dx == 1 else pl.ds(0, deep)
             place = pl.ds(4 - deep, deep) if dx == 1 else pl.ds(12, deep)
             for core in range(2):
-                send(field.at[part, pl.ds(24 if core == 0 else 0, 8), :],
-                     target.at[place, g, pl.ds(8 if core == 0 else 32, 8), :], ss, rs,
-                     (near_x(dx), near_y(1 if core == 0 else -1), core))
-                send(field.at[part, pl.ds(8 * core, 24), :],
-                     target.at[place, g, pl.ds(16 - 8 * core, 24), :], ss, rs, (near_x(dx), j, core))
-    for index, (field, target) in enumerate(((beta, C), (src, S))):
-        ss, rs = e1s.at[index], e1r.at[2 * index]
-        for core in range(2):
-            send(field.at[:, pl.ds(24 if core == 0 else 0, 8), :],
-                 target.at[pl.ds(4, 8), g, pl.ds(8 if core == 0 else 32, 8), :], ss, rs,
-                 (i, near_y(1 if core == 0 else -1), core))
+                send(field.at[part, pl.ds(8 * core, 24), :], target.at[place, g, pl.ds(16 - 8 * core, 24), :],
+                     e1s.at[index, 0], e1r.at[index, 0], (near_x(dx), j, core))
+    for index, (field, target, _) in enumerate(fields):
         send(field.at[:, pl.ds(pl.multiple_of(8 - 8 * g, 8), 24), :],
-             target.at[pl.ds(4, 8), g, pl.ds(pl.multiple_of(8 + 8 * g, 8), 24), :], ss, rs, (i, j, 1 - g))
-
-    def cells(count):
-        return C.at[pl.ds(0, count), :, pl.ds(0, 32), :]
+             target.at[pl.ds(4, 8), g, pl.ds(pl.multiple_of(8 + 8 * g, 8), 24), :],
+             e1s.at[index, 1], e1r.at[index, 1], (i, j, 1 - g))
+    for core, there, theirs, ours in ((0, up, 8, 24), (1, down, 32, 0)):
+
+        @pl.when(there)
+        def _():
+            far_y = near_y(1 - 2 * core)
+            for index, (field, target, _) in enumerate(fields):
+                send(field.at[:, pl.ds(ours, 8), :], target.at[pl.ds(4, 8), g, pl.ds(theirs, 8), :],
+                     e1s.at[index, 2 + core], e1r.at[index, 2], (i, far_y, core))
+            for index, (field, target, deep) in enumerate(fields):
+                for dx in (1, -1):
+                    part = pl.ds(8 - deep, deep) if dx == 1 else pl.ds(0, deep)
+                    place = pl.ds(4 - deep, deep) if dx == 1 else pl.ds(12, deep)
+                    send(field.at[part, pl.ds(ours, 8), :], target.at[place, g, pl.ds(theirs, 8), :],
+                         e1s.at[index, 4 + core], e1r.at[index, 3], (near_x(dx), far_y, core))
+
+    def outside(edge, row):
+        @pl.when(edge)
+        def _():
+            for field in (C, S):
+                field[:, :, pl.ds(row, 8), :] = jnp.zeros((16, 2, 8, 128), F32)
+
+    outside((j == 0) & (g == 0), 8)
+    outside((j == n_gy - 1) & (g == 1), 32)
+
+    def cells(layers, rows, tiles=2):
+        return C.at[pl.ds(0, layers), pl.ds(0, tiles), pl.ds(0, rows), :]
 
     wait(beta.at[:, pl.ds(0, 24), :], local.at[0])
-    wait(cells(5), e1r.at[0])
-
-    @pl.when((j == 0) & (g == 0))
-    def _():
-        C[pl.ds(4, 8), :, pl.ds(8, 8), :] = jnp.zeros((8, 2, 8, 128), F32)
-
-    @pl.when((j == n_gy - 1) & (g == 1))
-    def _():
-        C[pl.ds(4, 8), :, pl.ds(32, 8), :] = jnp.zeros((8, 2, 8, 128), F32)
+    wait(cells(8, 24, 1), e1r.at[0, 1])
+
+    @pl.when(has_side)
+    def _():
+        wait(cells(8, 8), e1r.at[0, 2])
 
     def mid_coefficient(m, _):
         for t in range(2):
@@ -222,7 +239,12 @@
     tell(1)
 
     wait(src.at[:, pl.ds(0, 24), :], local.at[1])
-    wait(cells(5), e1r.at[2])
+    wait(cells(8, 24, 1), e1r.at[1, 1])
+
+    @pl.when(has_side)
+    def _():
+        wait(cells(8, 8), e1r.at[1, 2])
+
 
     def fine_first(x, _):
         make_faces(x, C, fine, 8, 32, 1)
@@ -235,7 +257,12 @@
     layers(5, 11, fine_first)
     layers(6, 10, fine_second)
 
-    wait(cells(6), e1r.at[1])
+    wait(cells(6, 24), e1r.at[0, 0])
+
+    @pl.when(has_side)
+    def _():
+        wait(cells(6, 8), e1r.at[0, 3])
+
 
     @pl.when(i == 0)
     def _():
@@ -245,17 +272,12 @@
     def _():
         C[pl.ds(12, 3)] = jnp.zeros((3, *C.shape[1:]), F32)
 
-    @pl.when((j == 0) & (g == 0))
-    def _():
-        for low in (1, 12):
-            C[pl.ds(low, 3), :, pl.ds(8, 8), :] = jnp.zeros((3, 2, 8, 128), F32)
-
-    @pl.when((j == n_gy - 1) & (g == 1))
-    def _():
-        for low in (1, 12):
-            C[pl.ds(low, 3), :, pl.ds(32, 8), :] = jnp.zeros((3, 2, 8, 128), F32)
-
-    wait(cells(4), e1r.at[3])
+    wait(cells(4, 24), e1r.at[1, 0])
+
+    @pl.when(has_side)
+    def _():
+        wait(cells(4, 8), e1r.at[1, 3])
+
     layers(2, 5, fine_first)
     layers(11, 14, fine_first)
     last_face(14, C, fine, 8, 32)
@@ -344,12 +366,21 @@
     for m in range(4):
         for t in range(2):
             SY[m, t] = M2[3 + m, t, pl.ds(12, 8), :]
-    send(SY, Y2.at[g], ys, yr, (i, j, 1 - g))
-    send(SY, Y2.at[1 - g], ys, yr, (i, near_y(side), 1 - g))
+    send(SY, Y2.at[g], ys.at[0], yr.at[0], (i, j, 1 - g))
+
+    @pl.when(has_side)
+    def _():
+        send(SY, Y2.at[1 - g], ys.at[1], yr.at[1], (i, near_y(side), 1 - g))
+
     for m in range(4):
         for t in range(2):
             M2P[3 + m, t, mid_rows, :] = M2[3 + m, t, mid_rows, :]
-    wait(Y2, yr)
+    wait(Y2.at[0], yr.at[0])
+
+    @pl.when(has_side)
+    def _():
+        wait(Y2.at[0], yr.at[1])
+
     for m in range(4):
         for t in range(2):
             M2P[3 + m, t, pl.ds(9, 1), :] = Y2[0, m, t, pl.ds(5, 1), :]
@@ -441,11 +472,19 @@
 
     for b in range(3):
         SQ[b] = low[b]
-    send(SQ, Q.at[:, pl.ds(pl.multiple_of(16 - 16 * g, 8), 8), :], qs, qr, (i, near_y(side), 1 - g))
+
+    @pl.when(has_side)
+    def _():
+        send(SQ, Q.at[:, pl.ds(pl.multiple_of(16 - 16 * g, 8), 8), :], qs, qr, (i, near_y(side), 1 - g))
+
     for b in range(3):
         Q[b, pl.ds(8, 8), :] = low[b]
     wait(M2P.at[pl.ds(0, 6), :, mid_rows, :], xr)
-    wait(SQ, qr)
+
+    @pl.when(has_side)
+    def _():
+        wait(SQ, qr)
+
     for b in range(3):
         fix = jnp.where(g == 0, Q[b, pl.ds(6, 8), :], Q[b, pl.ds(10, 8), :])
         for part, wide in enumerate(unbraid(fix)):
@@ -494,17 +533,31 @@
     keep = pltpu.make_async_copy(FO.at[:, g], out.at[:, out_rows, :], local.at[2])
     keep.start()
 
-    wait(cells(11), e1s.at[0])
-    wait(cells(9), e1s.at[1])
+    for index, deep in ((0, 3), (1, 2)):
+        wait(cells(2 * deep, 24), e1s.at[index, 0])
+        wait(cells(8, 24, 1), e1s.at[index, 1])
+    for core, there in ((0, up), (1, down)):
+
+        @pl.when(there)
+        def _():
+            for index, deep in ((0, 3), (1, 2)):
+                wait(cells(8, 8, 1), e1s.at[index, 2 + core])
+                wait(cells(2 * deep, 8, 1), e1s.at[index, 4 + core])
+
     wait(V2.at[pl.ds(0, 2), :, fine_rows, :], vs)
     wait(MC.at[pl.ds(0, 6), :, mid_rows, :], mcs)
     wait(MS.at[pl.ds(0, 4), :, mid_rows, :], mss)
     wait(EB.at[pl.ds(0, 17)], ebs)
     wait(GB.at[pl.ds(0, 17)], gs)
     wait(FB, fs)
-    wait(Y2, ys)
+    wait(Y2.at[0], ys.at[0])
     wait(M2P.at[pl.ds(0, 6), :, mid_rows, :], xs)
-    wait(SQ, qs)
+
+    @pl.when(has_side)
+    def _():
+        wait(Y2.at[0], ys.at[1])
+        wait(SQ, qs)
+
     keep.wait()
     wait(FO.at[:, 0], os_)
     wait(out.at[:, pl.ds(0, 16), :], or_)
@@ -551,9 +604,12 @@
                 pltpu.VMEM((6, 2, 32, 128), F32),
                 pltpu.VMEM((8, 2, 16, 128), F32),
                 dma((3,)),
+                dma((2, 6)),
+                dma((2, 4)),
+                *[dma] * 10,
                 dma((2,)),
-                dma((4,)),
-                *[dma] * 19,
+                dma((2,)),
+                *[dma] * 7,
                 dma((2,)),
                 pltpu.SemaphoreType.REGULAR((2,)),
             ],

time: 43 us -> 39.5 us (0.919)
  the two profiles are of different devices: /device:TPU:1 before, /device:TPU:25 now
where the time goes in v4:
time: 39.5 us; the launch traced here: 39.3 us
  Pallas kernels  36.2 us (92%)
  local copies, waits for them, and re-layouts  2.46 us (6%)
  between operations  0.67 us (2%)
    pallas_call x1, Pallas kernels, per_device(): pl.pallas_call(kernel, out_shape=jax.ShapeDtypeStruct(source.shape, F32),...  36.2 us
    unnamed x5, local copies, waits for them, and re-layouts  2.46 us

profile of v4, /device:TPU:25, one launch (start us, length us, event | category | flops | bytes accessed | tf_op | source)
XLA Modules:
  0.0 39.3 jit_solution(17394798699063328071)
XLA Ops:
  0.7 0.0 copy-start
  0.7 0.9 %copy-done = f32[8,32,128]{2,1,0:T(8,128)S(1)} copy-done((f32[8,32,128]{2,1,0:T(8,128)S(1)}, f32[8,32,128]{2,1,0:T(8,128)}, u32[]{:S(2)}) %copy-start) | copy-done | bytes 131096
  1.6 0.0 copy-start.1
  1.6 0.9 %copy-done.1 = f32[8,32,128]{2,1,0:T(8,128)S(1)} copy-done((f32[8,32,128]{2,1,0:T(8,128)S(1)}, f32[8,32,128]{2,1,0:T(8,128)}, u32[]{:S(2)}) %copy-start.1) | copy-done | bytes 131096
  2.5 36.2 %cycle.1 = f32[8,32,128]{2,1,0:T(8,128)S(1)} custom-call(f32[8,32,128]{2,1,0:T(8,128)S(1)} %copy-done, f32[8,32,128]{2,1,0:T(8,128)S(1)} %copy-done.1, s32[1,1,1]{2,1,0:T(1,128)S(6)} %copy.5.refs_2_), custom_call_target="tpu_custom_call" | custom-call | tf_op jit(solution)/shard_map/cycle/pallas_call | solution.py:577
  38.7 0.7 %copy.6 = f32[8,32,128]{2,1,0:T(8,128)} copy(f32[8,32,128]{2,1,0:T(8,128)S(1)} %cycle.1) | data formatting | bytes 262144
Async XLA Ops:
  0.7 0.9 %copy-start = (f32[8,32,128]{2,1,0:T(8,128)S(1)}, f32[8,32,128]{2,1,0:T(8,128)}, u32[]{:S(2)}) copy-start(f32[8,32,128]{2,1,0:T(8,128)} %refs_0_.1) | copy-start | bytes 393220
  1.6 0.9 %copy-start.1 = (f32[8,32,128]{2,1,0:T(8,128)S(1)}, f32[8,32,128]{2,1,0:T(8,128)}, u32[]{:S(2)}) copy-start(f32[8,32,128]{2,1,0:T(8,128)} %refs_1_.1) | copy-start | bytes 393220

commit v5 on v4

--- a/solution.py
+++ b/solution.py
@@ -126,8 +126,8 @@
 def cycle(n_gx, n_gy, src, beta, tgt, out, *scratch):
     (C, S, FX, FY, FL, FR, W, E, V1, V2, V3,
      MC, MS, MFX, MFY, MFL, MFR, MW, ME, M1, M2, M2P, M3, M4,
-     RS, RC, R2, SY, Y2, SX, EB, ES, GB, GS, FB, FS, Q, SQ, PK, PF, FO,
-     local, e1s, e1r, mcs, mcr, mss, msr, ebs, ebr, gs, gr, fs, fr, ys, yr, xs, xr, qs, qr, os_, or_, vs, vr, known) = scratch
+     RS, RC, R2, SY, Y2, SX, EB, ES, GB, GS, FB, Q, SQ, PK, PF, FO,
+     local, e1s, e1r, mcs, mcr, mss, msr, ebs, ebr, gs, gr, fs, fr, ys, yr, xs, xr, qs, qr, os_, or_, vs, vr, ebss, ebsr, gss, gsr, ts, tr, TS, TB, QP, known) = scratch
     i, j, g = lax.axis_index("gx"), lax.axis_index("gy"), lax.axis_index("gz")
     fine = (FX, FY, FL, FR, W, E)
     mid = (MFX, MFY, MFL, MFR, MW, ME)
@@ -144,9 +144,9 @@
             device_id=where, device_id_type=MESH,
         ).start()
 
-    def tell(step):
+    def tell():
         for sign in (1, -1):
-            pl.semaphore_signal(known.at[step], inc=1, device_id=(near_x(sign * 3), j, g), device_id_type=MESH)
+            pl.semaphore_signal(known.at[0], inc=1, device_id=(near_x(sign * 4), j, g), device_id_type=MESH)
 
     def wait(ref, sem):
         pltpu.make_async_copy(ref, ref, sem).wait()
@@ -170,15 +170,30 @@
             for core in range(2):
                 greet((near_x(dx), near_y(side), core))
 
-    for dx in (3, 2, 1):
+    for dx in (4, 3, 2, 1):
         for sign in (1, -1):
-            for core in range(2 if dx < 3 else 1):
-                greet((near_x(sign * dx), j, core if dx < 3 else g))
+            for core in range(2 if dx == 1 else 1):
+                greet((near_x(sign * dx), j, core if dx == 1 else g))
     greet((i, j, 1 - g))
     pl.semaphore_wait(barrier, 11 + 3 * (up.astype(jnp.int32) + down.astype(jnp.int32)))
-    tell(0)
+    tell()
 
     fields = ((beta, C, 3), (src, S, 2))
+    for core, there, theirs, ours in ((0, up, 8, 24), (1, down, 32, 0)):
+
+        @pl.when(there)
+        def _():
+            far_y = near_y(1 - 2 * core)
+            for index, (field, target, deep) in enumerate(fields):
+                for dx in (1, -1):
+                    part = pl.ds(8 - deep, deep) if dx == 1 else pl.ds(0, deep)
+                    place = pl.ds(4 - deep, deep) if dx == 1 else pl.ds(12, deep)
+                    send(field.at[part, pl.ds(ours, 8), :], target.at[place, g, pl.ds(theirs, 8), :],
+                         e1s.at[index, 4 + core], e1r.at[index, 3], (near_x(dx), far_y, core))
+            for index, (field, target, _) in enumerate(fields):
+                send(field.at[:, pl.ds(ours, 8), :], target.at[pl.ds(4, 8), g, pl.ds(theirs, 8), :],
+                     e1s.at[index, 2 + core], e1r.at[index, 2], (i, far_y, core))
+
     for index, (field, target, deep) in enumerate(fields):
         for dx in (1, -1):
             part = pl.ds(8 - deep, deep) if dx == 1 else pl.ds(0, deep)
@@ -190,21 +205,6 @@
         send(field.at[:, pl.ds(pl.multiple_of(8 - 8 * g, 8), 24), :],
              target.at[pl.ds(4, 8), g, pl.ds(pl.multiple_of(8 + 8 * g, 8), 24), :],
              e1s.at[index, 1], e1r.at[index, 1], (i, j, 1 - g))
-    for core, there, theirs, ours in ((0, up, 8, 24), (1, down, 32, 0)):
-
-        @pl.when(there)
-        def _():
-            far_y = near_y(1 - 2 * core)
-            for index, (field, target, _) in enumerate(fields):
-                send(field.at[:, pl.ds(ours, 8), :], target.at[pl.ds(4, 8), g, pl.ds(theirs, 8), :],
-                     e1s.at[index, 2 + core], e1r.at[index, 2], (i, far_y, core))
-            for index, (field, target, deep) in enumerate(fields):
-                for dx in (1, -1):
-                    part = pl.ds(8 - deep, deep) if dx == 1 else pl.ds(0, deep)
-                    place = pl.ds(4 - deep, deep) if dx == 1 else pl.ds(12, deep)
-                    send(field.at[part, pl.ds(ours, 8), :], target.at[place, g, pl.ds(theirs, 8), :],
-                         e1s.at[index, 4 + core], e1r.at[index, 3], (near_x(dx), far_y, core))
-
     def outside(edge, row):
         @pl.when(edge)
         def _():
@@ -236,7 +236,10 @@
     send(MC.at[pl.ds(3, 3), :, mid_rows, :], MC.at[pl.ds(7, 3), :, mid_rows, :], mcs, mcr, (near_x(-1), j, g))
 
     pl.semaphore_wait(known.at[0], 2)
-    tell(1)
+
+    @pl.when(has_side)
+    def _():
+        pl.semaphore_signal(known.at[1], inc=1, device_id=(i, near_y(side), 1 - g), device_id_type=MESH)
 
     wait(src.at[:, pl.ds(0, 24), :], local.at[1])
     wait(cells(8, 24, 1), e1r.at[1, 1])
@@ -317,7 +320,7 @@
         for sign in (1, -1):
             for core in range(2):
                 send(ES, EB.at[2 * (NEAR - sign * d) + g], ebs, ebr, (near_x(sign * d), j, core))
-    send(ES, EB.at[2 * NEAR + g], ebs, ebr, (i, j, 1 - g))
+    send(ES, EB.at[2 * NEAR + g], ebss, ebsr, (i, j, 1 - g))
 
     wait(MC.at[pl.ds(0, 6), :, mid_rows, :], mcr)
 
@@ -349,29 +352,42 @@
     mid_res = [left_over(3 + m, M2, mid, MS, 0.125, 8, 16, 2) for m in range(4)]
     low_src = coarsest(lambda m, t: mid_res[m][t], 0.125)
 
-    pl.semaphore_wait(known.at[1], 2)
     GS[...] = low_src
-    FS[pl.ds(0, 1), :] = jnp.sum(low_src, axis=0, keepdims=True)
-    FS[pl.ds(1, 1), :] = own_target[:1]
     GB[2 * NEAR + g] = low_src
-    for d in sorted(range(NEAR + 1, n_gx - NEAR), key=lambda d: -min(d, n_gx - d)):
-        for core in range(2):
-            send(FS, FB.at[2 * (n_gx - d - NEAR - 1) + g], fs, fr, (near_x(d), j, core))
+    send(GS, GB.at[2 * NEAR + g], gss, gsr, (i, j, 1 - g))
     for d in (4, 3, 2, 1):
         for sign in (1, -1):
             for core in range(2):
                 send(GS, GB.at[2 * (NEAR - sign * d) + g], gs, gr, (near_x(sign * d), j, core))
-    send(GS, GB.at[2 * NEAR + g], gs, gr, (i, j, 1 - g))
+    wait(GB.at[0], gsr)
+
+    wait(EB.at[0], ebsr)
+    halves = [EB[2 * NEAR + core][4:5] for core in range(2)]
+    TS[pl.ds(0, 1), :] = jnp.sum(low_src + GB[2 * NEAR + 1 - g], axis=0, keepdims=True)
+    TS[pl.ds(1, 1), :] = jnp.where(lanes_of(1) % 2 == 0, halves[0], halves[1])
+
+    @pl.when(has_side)
+    def _():
+        pl.semaphore_wait(known.at[1], 1)
+
+    far_y = near_y(side)
+    for d in sorted(range(NEAR + 1, n_gx - NEAR), key=lambda d: -min(d, n_gx - d)):
+        slot = n_gx - d - NEAR - 1
+
+        @pl.when(has_side)
+        def _():
+            send(TS, TB.at[slot], ts, tr, (near_x(d), far_y, 1 - g))
+
+        send(TS, FB.at[slot], fs, fr, (near_x(d), j, g))
 
     for m in range(4):
         for t in range(2):
             SY[m, t] = M2[3 + m, t, pl.ds(12, 8), :]
+    @pl.when(has_side)
+    def _():
+        send(SY, Y2.at[1 - g], ys.at[1], yr.at[1], (i, near_y(side), 1 - g))
+
     send(SY, Y2.at[g], ys.at[0], yr.at[0], (i, j, 1 - g))
-
-    @pl.when(has_side)
-    def _():
-        send(SY, Y2.at[1 - g], ys.at[1], yr.at[1], (i, near_y(side), 1 - g))
-
     for m in range(4):
         for t in range(2):
             M2P[3 + m, t, mid_rows, :] = M2[3 + m, t, mid_rows, :]
@@ -388,7 +404,7 @@
     send(M2P.at[pl.ds(4, 3), :, mid_rows, :], M2P.at[pl.ds(0, 3), :, mid_rows, :], xs, xr, (near_x(1), j, g))
     send(M2P.at[pl.ds(3, 3), :, mid_rows, :], M2P.at[pl.ds(7, 3), :, mid_rows, :], xs, xr, (near_x(-1), j, g))
 
-    wait(EB.at[pl.ds(0, 17)], ebr)
+    wait(EB.at[pl.ds(0, 16)], ebr)
     lane = lanes_of(8)
     row = lax.broadcasted_iota(jnp.int32, (8, 128), 0)
     layer, tile, cell = (lane % 4) // 2, lane % 2, lane // 4
@@ -445,45 +461,59 @@
         return low[NEAR - 1:NEAR + 2]
 
     from_mean = solve([jnp.full((8, 128), 4.0, F32)] * boxes, None)
-    wait(GB.at[pl.ds(0, 17)], gr)
+    wait(GB.at[pl.ds(0, 16)], gr)
     rhs = [jnp.concatenate([GB[2 * b], GB[2 * b + 1]], axis=0) for b in range(boxes)]
     from_source = solve([zero] * boxes, rhs)
     sums = [jnp.sum(v, axis=0, keepdims=True) for v in rhs]
+    for b in range(3):
+        SQ[b] = from_source[b]
+        SQ[3 + b] = from_mean[b]
+    for b in range(boxes):
+        SQ[6 + b // 8, pl.ds(b % 8, 1), :] = sums[b]
+        SQ[8 + b // 8, pl.ds(b % 8, 1), :] = marks[b][:1]
+
+    @pl.when(has_side)
+    def _():
+        send(SQ, QP, qs, qr, (i, near_y(side), 1 - g))
+
     names = [m[:1] for m in marks]
-    top_tile = tile[:1]
     src_lane = lax.broadcasted_iota(jnp.int32, (128, 128), 0)
     dst_lane = lax.broadcasted_iota(jnp.int32, (128, 128), 1)
     same_tile = jnp.where(src_lane % 2 == dst_lane % 2, 1.0, 0.0).astype(F32)
 
     wait(FB, fr)
     for d in range(n_gx - boxes):
-        first, second = FB[2 * d], FB[2 * d + 1]
-        sums.append(first[:1] + second[:1])
-        names.append(jnp.where(top_tile == 0, first[1:], second[1:]))
+        sums.append(FB[d][:1])
+        names.append(FB[d][1:])
+    @pl.when(has_side)
+    def _():
+        wait(TB, tr)
+        wait(SQ, qr)
+
+    for b in range(boxes):
+        sums.append(QP[6 + b // 8, pl.ds(b % 8, 1), :])
+        names.append(QP[8 + b // 8, pl.ds(b % 8, 1), :])
+    for d in range(n_gx - boxes):
+        sums.append(TB[d][:1])
+        names.append(TB[d][1:])
     sums = exact_dot(jnp.concatenate(sums, axis=0), same_tile)
     names = jnp.concatenate(names, axis=0)
-    low = []
-    for b in range(3):
-        here = NEAR - 1 + b
-        same = names == names[here:here + 1]
-        total = jnp.sum(jnp.where(same, sums, 0.0), axis=0, keepdims=True)
-        number = jnp.sum(jnp.where(same, 512.0, 0.0), axis=0, keepdims=True)
-        low.append(from_source[b] + (total / jnp.maximum(number, 1.0)) * from_mean[b])
-
-    for b in range(3):
-        SQ[b] = low[b]
-
-    @pl.when(has_side)
-    def _():
-        send(SQ, Q.at[:, pl.ds(pl.multiple_of(16 - 16 * g, 8), 8), :], qs, qr, (i, near_y(side), 1 - g))
-
-    for b in range(3):
-        Q[b, pl.ds(8, 8), :] = low[b]
+
+    def means(first):
+        row_sums, row_names = sums[first:first + n_gx], names[first:first + n_gx]
+        for place in (NEAR - 1, NEAR, NEAR + 1):
+            same = row_names == row_names[place:place + 1]
+            total = jnp.sum(jnp.where(same, row_sums, 0.0), axis=0, keepdims=True)
+            number = jnp.sum(jnp.where(same, 512.0, 0.0), axis=0, keepdims=True)
+            yield total / jnp.maximum(number, 1.0)
+
+    side_at = pl.ds(pl.multiple_of(16 * g, 8), 8)
+    for b, mean in enumerate(means(0)):
+        Q[b, pl.ds(8, 8), :] = from_source[b] + mean * from_mean[b]
+    for b, mean in enumerate(means(n_gx)):
+        Q[b, side_at, :] = QP[b] + mean * QP[3 + b]
+
     wait(M2P.at[pl.ds(0, 6), :, mid_rows, :], xr)
-
-    @pl.when(has_side)
-    def _():
-        wait(SQ, qr)
 
     for b in range(3):
         fix = jnp.where(g == 0, Q[b, pl.ds(6, 8), :], Q[b, pl.ds(10, 8), :])
@@ -547,8 +577,10 @@
     wait(V2.at[pl.ds(0, 2), :, fine_rows, :], vs)
     wait(MC.at[pl.ds(0, 6), :, mid_rows, :], mcs)
     wait(MS.at[pl.ds(0, 4), :, mid_rows, :], mss)
-    wait(EB.at[pl.ds(0, 17)], ebs)
-    wait(GB.at[pl.ds(0, 17)], gs)
+    wait(EB.at[pl.ds(0, 16)], ebs)
+    wait(EB.at[0], ebss)
+    wait(GB.at[pl.ds(0, 16)], gs)
+    wait(GB.at[0], gss)
     wait(FB, fs)
     wait(Y2.at[0], ys.at[0])
     wait(M2P.at[pl.ds(0, 6), :, mid_rows, :], xs)
@@ -557,6 +589,7 @@
     def _():
         wait(Y2.at[0], ys.at[1])
         wait(SQ, qs)
+        wait(TB, ts)
 
     keep.wait()
     wait(FO.at[:, 0], os_)
@@ -596,10 +629,9 @@
                 pltpu.VMEM((8, 128), F32),
                 pltpu.VMEM((4 * NEAR + 2, 4, 128), F32),
                 pltpu.VMEM((4, 128), F32),
-                pltpu.VMEM((2 * far, 2, 128), F32),
-                pltpu.VMEM((2, 128), F32),
+                pltpu.VMEM((far, 2, 128), F32),
                 pltpu.VMEM((3, 24, 128), F32),
-                pltpu.VMEM((3, 8, 128), F32),
+                pltpu.VMEM((10, 8, 128), F32),
                 pltpu.VMEM((6, 2, 16, 128), F32),
                 pltpu.VMEM((6, 2, 32, 128), F32),
                 pltpu.VMEM((8, 2, 16, 128), F32),
@@ -611,6 +643,10 @@
                 dma((2,)),
                 *[dma] * 7,
                 dma((2,)),
+                *[dma] * 6,
+                pltpu.VMEM((2, 128), F32),
+                pltpu.VMEM((far, 2, 128), F32),
+                pltpu.VMEM((10, 8, 128), F32),
                 pltpu.SemaphoreType.REGULAR((2,)),
             ],
             compiler_params=pltpu.CompilerParams(

time: 39.5 us -> 38.6 us (0.977)
  Pallas kernels: 36.2 us -> 35.3 us
    pallas_call x1, Pallas kernels: 36.2 us -> 35.3 us  [per_device(): pl.pallas_call(kernel, out_shape=jax.ShapeDtypeStruct(source.shape, F32),...]
where the time goes in v5:
time: 38.6 us; the launch traced here: 38.5 us
  Pallas kernels  35.3 us (91%)
  local copies, waits for them, and re-layouts  2.46 us (6%)
  between operations  0.67 us (2%)
    pallas_call x1, Pallas kernels, per_device(): pl.pallas_call(kernel, out_shape=jax.ShapeDtypeStruct(source.shape, F32),...  35.3 us
    unnamed x5, local copies, waits for them, and re-layouts  2.46 us

profile of v5, /device:TPU:25, one launch (start us, length us, event | category | flops | bytes accessed | tf_op | source)
XLA Modules:
  0.0 38.5 jit_solution(11583767606053854364)
XLA Ops:
  0.7 0.0 copy-start
  0.7 0.9 %copy-done = f32[8,32,128]{2,1,0:T(8,128)S(1)} copy-done((f32[8,32,128]{2,1,0:T(8,128)S(1)}, f32[8,32,128]{2,1,0:T(8,128)}, u32[]{:S(2)}) %copy-start) | copy-done | bytes 131096
  1.6 0.0 copy-start.1
  1.6 0.9 %copy-done.1 = f32[8,32,128]{2,1,0:T(8,128)S(1)} copy-done((f32[8,32,128]{2,1,0:T(8,128)S(1)}, f32[8,32,128]{2,1,0:T(8,128)}, u32[]{:S(2)}) %copy-start.1) | copy-done | bytes 131096
  2.5 35.3 %cycle.1 = f32[8,32,128]{2,1,0:T(8,128)S(1)} custom-call(f32[8,32,128]{2,1,0:T(8,128)S(1)} %copy-done, f32[8,32,128]{2,1,0:T(8,128)S(1)} %copy-done.1, s32[1,1,1]{2,1,0:T(1,128)S(6)} %copy.5.refs_2_), custom_call_target="tpu_custom_call" | custom-call | tf_op jit(solution)/shard_map/cycle/pallas_call | solution.py:610
  37.8 0.7 %copy.6 = f32[8,32,128]{2,1,0:T(8,128)} copy(f32[8,32,128]{2,1,0:T(8,128)S(1)} %cycle.1) | data formatting | bytes 262144
Async XLA Ops:
  0.7 0.9 %copy-start = (f32[8,32,128]{2,1,0:T(8,128)S(1)}, f32[8,32,128]{2,1,0:T(8,128)}, u32[]{:S(2)}) copy-start(f32[8,32,128]{2,1,0:T(8,128)} %refs_0_.1) | copy-start | bytes 393220
  1.6 0.9 %copy-start.1 = (f32[8,32,128]{2,1,0:T(8,128)S(1)}, f32[8,32,128]{2,1,0:T(8,128)}, u32[]{:S(2)}) copy-start(f32[8,32,128]{2,1,0:T(8,128)} %refs_1_.1) | copy-start | bytes 393220

commit v6 on v5

--- a/solution.py
+++ b/solution.py
@@ -235,12 +235,6 @@
     send(MC.at[pl.ds(4, 3), :, mid_rows, :], MC.at[pl.ds(0, 3), :, mid_rows, :], mcs, mcr, (near_x(1), j, g))
     send(MC.at[pl.ds(3, 3), :, mid_rows, :], MC.at[pl.ds(7, 3), :, mid_rows, :], mcs, mcr, (near_x(-1), j, g))
 
-    pl.semaphore_wait(known.at[0], 2)
-
-    @pl.when(has_side)
-    def _():
-        pl.semaphore_signal(known.at[1], inc=1, device_id=(i, near_y(side), 1 - g), device_id_type=MESH)
-
     wait(src.at[:, pl.ds(0, 24), :], local.at[1])
     wait(cells(8, 24, 1), e1r.at[1, 1])
 
@@ -259,6 +253,12 @@
 
     layers(5, 11, fine_first)
     layers(6, 10, fine_second)
+
+    pl.semaphore_wait(known.at[0], 2)
+
+    @pl.when(has_side)
+    def _():
+        pl.semaphore_signal(known.at[1], inc=1, device_id=(i, near_y(side), 1 - g), device_id_type=MESH)
 
     wait(cells(6, 24), e1r.at[0, 0])
 
@@ -359,6 +359,18 @@
         for sign in (1, -1):
             for core in range(2):
                 send(GS, GB.at[2 * (NEAR - sign * d) + g], gs, gr, (near_x(sign * d), j, core))
+    for m in range(6):
+        for t in range(2):
+            SY[m, t] = M2[2 + m, t, pl.ds(12, 8), :]
+
+    @pl.when(has_side)
+    def _():
+        send(SY, Y2.at[1 - g], ys.at[1], yr.at[1], (i, near_y(side), 1 - g))
+
+    send(SY, Y2.at[g], ys.at[0], yr.at[0], (i, j, 1 - g))
+    send(M2.at[pl.ds(4, 2), :, mid_rows, :], M2P.at[pl.ds(0, 2), :, mid_rows, :], xs, xr, (near_x(1), j, g))
+    send(M2.at[pl.ds(4, 2), :, mid_rows, :], M2P.at[pl.ds(8, 2), :, mid_rows, :], xs, xr, (near_x(-1), j, g))
+
     wait(GB.at[0], gsr)
 
     wait(EB.at[0], ebsr)
@@ -379,30 +391,6 @@
             send(TS, TB.at[slot], ts, tr, (near_x(d), far_y, 1 - g))
 
         send(TS, FB.at[slot], fs, fr, (near_x(d), j, g))
-
-    for m in range(4):
-        for t in range(2):
-            SY[m, t] = M2[3 + m, t, pl.ds(12, 8), :]
-    @pl.when(has_side)
-    def _():
-        send(SY, Y2.at[1 - g], ys.at[1], yr.at[1], (i, near_y(side), 1 - g))
-
-    send(SY, Y2.at[g], ys.at[0], yr.at[0], (i, j, 1 - g))
-    for m in range(4):
-        for t in range(2):
-            M2P[3 + m, t, mid_rows, :] = M2[3 + m, t, mid_rows, :]
-    wait(Y2.at[0], yr.at[0])
-
-    @pl.when(has_side)
-    def _():
-        wait(Y2.at[0], yr.at[1])
-
-    for m in range(4):
-        for t in range(2):
-            M2P[3 + m, t, pl.ds(9, 1), :] = Y2[0, m, t, pl.ds(5, 1), :]
-            M2P[3 + m, t, pl.ds(22, 1), :] = Y2[1, m, t, pl.ds(2, 1), :]
-    send(M2P.at[pl.ds(4, 3), :, mid_rows, :], M2P.at[pl.ds(0, 3), :, mid_rows, :], xs, xr, (near_x(1), j, g))
-    send(M2P.at[pl.ds(3, 3), :, mid_rows, :], M2P.at[pl.ds(7, 3), :, mid_rows, :], xs, xr, (near_x(-1), j, g))
 
     wait(EB.at[pl.ds(0, 16)], ebr)
     lane = lanes_of(8)
@@ -445,8 +433,8 @@
         low_faces.append(faces[:2] + [jnp.where(keep, f, 0.0) for keep, f in zip(keeps, faces[2:])])
         low_ease.append(RELAX / total)
 
-    def solve(low, rhs):
-        for number in range(BOTTOM):
+    def solve(low, rhs, sweeps):
+        for number in range(sweeps):
             below, above = along_x(low)
             fresh = []
             for b in range(boxes):
@@ -460,10 +448,10 @@
             low = fresh
         return low[NEAR - 1:NEAR + 2]
 
-    from_mean = solve([jnp.full((8, 128), 4.0, F32)] * boxes, None)
+    from_mean = solve([jnp.full((8, 128), 4.0, F32)] * boxes, None, BOTTOM)
     wait(GB.at[pl.ds(0, 16)], gr)
     rhs = [jnp.concatenate([GB[2 * b], GB[2 * b + 1]], axis=0) for b in range(boxes)]
-    from_source = solve([zero] * boxes, rhs)
+    from_source = solve([low_ease[b] * (32.0 * rhs[b]) for b in range(boxes)], rhs, BOTTOM - 1)
     sums = [jnp.sum(v, axis=0, keepdims=True) for v in rhs]
     for b in range(3):
         SQ[b] = from_source[b]
@@ -476,6 +464,19 @@
     def _():
         send(SQ, QP, qs, qr, (i, near_y(side), 1 - g))
 
+    for m in range(6):
+        for t in range(2):
+            M2P[2 + m, t, mid_rows, :] = M2[2 + m, t, mid_rows, :]
+    wait(Y2.at[0], yr.at[0])
+
+    @pl.when(has_side)
+    def _():
+        wait(Y2.at[0], yr.at[1])
+
+    for m in range(6):
+        for t in range(2):
+            M2P[2 + m, t, pl.ds(9, 1), :] = Y2[0, m, t, pl.ds(5, 1), :]
+            M2P[2 + m, t, pl.ds(22, 1), :] = Y2[1, m, t, pl.ds(2, 1), :]
     names = [m[:1] for m in marks]
     src_lane = lax.broadcasted_iota(jnp.int32, (128, 128), 0)
     dst_lane = lax.broadcasted_iota(jnp.int32, (128, 128), 1)
@@ -513,7 +514,7 @@
     for b, mean in enumerate(means(n_gx)):
         Q[b, side_at, :] = QP[b] + mean * QP[3 + b]
 
-    wait(M2P.at[pl.ds(0, 6), :, mid_rows, :], xr)
+    wait(M2P.at[pl.ds(0, 4), :, mid_rows, :], xr)
 
     for b in range(3):
         fix = jnp.where(g == 0, Q[b, pl.ds(6, 8), :], Q[b, pl.ds(10, 8), :])
@@ -583,7 +584,7 @@
     wait(GB.at[0], gss)
     wait(FB, fs)
     wait(Y2.at[0], ys.at[0])
-    wait(M2P.at[pl.ds(0, 6), :, mid_rows, :], xs)
+    wait(M2P.at[pl.ds(0, 4), :, mid_rows, :], xs)
 
     @pl.when(has_side)
     def _():
@@ -622,8 +623,8 @@
                 pltpu.VMEM((4, 2, 32, 128), F32),
                 pltpu.VMEM((4, 2, 32, 128), F32),
                 pltpu.VMEM((2, 2, 16, 128), F32),
-                pltpu.VMEM((4, 2, 8, 128), F32),
-                pltpu.VMEM((2, 4, 2, 8, 128), F32),
+                pltpu.VMEM((6, 2, 8, 128), F32),
+                pltpu.VMEM((2, 6, 2, 8, 128), F32),
                 pltpu.VMEM((8, 128), F32),
                 pltpu.VMEM((4 * NEAR + 2, 8, 128), F32),
                 pltpu.VMEM((8, 128), F32),

time: 38.6 us -> 38.6 us (level)
  no operation moved by 1% of the time
where the time goes in v6:
time: 38.6 us; the launch traced here: 38.5 us
  Pallas kernels  35.3 us (91%)
  local copies, waits for them, and re-layouts  2.46 us (6%)
  between operations  0.67 us (2%)
    pallas_call x1, Pallas kernels, per_device(): pl.pallas_call(kernel, out_shape=jax.ShapeDtypeStruct(source.shape, F32),...  35.3 us
    unnamed x5, local copies, waits for them, and re-layouts  2.46 us

profile of v6, /device:TPU:25, one launch (start us, length us, event | category | flops | bytes accessed | tf_op | source)
XLA Modules:
  0.0 38.5 jit_solution(495369693435180254)
XLA Ops:
  0.7 0.0 copy-start
  0.7 0.9 %copy-done = f32[8,32,128]{2,1,0:T(8,128)S(1)} copy-done((f32[8,32,128]{2,1,0:T(8,128)S(1)}, f32[8,32,128]{2,1,0:T(8,128)}, u32[]{:S(2)}) %copy-start) | copy-done | bytes 131096
  1.6 0.0 copy-start.1
  1.6 0.9 %copy-done.1 = f32[8,32,128]{2,1,0:T(8,128)S(1)} copy-done((f32[8,32,128]{2,1,0:T(8,128)S(1)}, f32[8,32,128]{2,1,0:T(8,128)}, u32[]{:S(2)}) %copy-start.1) | copy-done | bytes 131096
  2.5 35.3 %cycle.1 = f32[8,32,128]{2,1,0:T(8,128)S(1)} custom-call(f32[8,32,128]{2,1,0:T(8,128)S(1)} %copy-done, f32[8,32,128]{2,1,0:T(8,128)S(1)} %copy-done.1, s32[1,1,1]{2,1,0:T(1,128)S(6)} %copy.5.refs_2_), custom_call_target="tpu_custom_call" | custom-call | tf_op jit(solution)/shard_map/cycle/pallas_call | solution.py:611
  37.8 0.7 %copy.6 = f32[8,32,128]{2,1,0:T(8,128)} copy(f32[8,32,128]{2,1,0:T(8,128)S(1)} %cycle.1) | data formatting | bytes 262144
Async XLA Ops:
  0.7 0.9 %copy-start = (f32[8,32,128]{2,1,0:T(8,128)S(1)}, f32[8,32,128]{2,1,0:T(8,128)}, u32[]{:S(2)}) copy-start(f32[8,32,128]{2,1,0:T(8,128)} %refs_0_.1) | copy-start | bytes 393220
  1.6 0.9 %copy-start.1 = (f32[8,32,128]{2,1,0:T(8,128)S(1)}, f32[8,32,128]{2,1,0:T(8,128)}, u32[]{:S(2)}) copy-start(f32[8,32,128]{2,1,0:T(8,128)} %refs_1_.1) | copy-start | bytes 393220

commit v7 on v6

--- a/solution.py
+++ b/solution.py
@@ -300,9 +300,6 @@
     send(MS.at[pl.ds(5, 2), :, mid_rows, :], MS.at[pl.ds(1, 2), :, mid_rows, :], mss, msr, (near_x(1), j, g))
     send(MS.at[pl.ds(3, 2), :, mid_rows, :], MS.at[pl.ds(7, 2), :, mid_rows, :], mss, msr, (near_x(-1), j, g))
 
-    send(V2.at[10, :, fine_rows, :], V2.at[2, :, fine_rows, :], vs, vr.at[0], (near_x(1), j, g))
-    send(V2.at[5, :, fine_rows, :], V2.at[13, :, fine_rows, :], vs, vr.at[1], (near_x(-1), j, g))
-
     def coarsest(field, scale):
         parts = []
         for layer in range(2):
@@ -359,18 +356,6 @@
         for sign in (1, -1):
             for core in range(2):
                 send(GS, GB.at[2 * (NEAR - sign * d) + g], gs, gr, (near_x(sign * d), j, core))
-    for m in range(6):
-        for t in range(2):
-            SY[m, t] = M2[2 + m, t, pl.ds(12, 8), :]
-
-    @pl.when(has_side)
-    def _():
-        send(SY, Y2.at[1 - g], ys.at[1], yr.at[1], (i, near_y(side), 1 - g))
-
-    send(SY, Y2.at[g], ys.at[0], yr.at[0], (i, j, 1 - g))
-    send(M2.at[pl.ds(4, 2), :, mid_rows, :], M2P.at[pl.ds(0, 2), :, mid_rows, :], xs, xr, (near_x(1), j, g))
-    send(M2.at[pl.ds(4, 2), :, mid_rows, :], M2P.at[pl.ds(8, 2), :, mid_rows, :], xs, xr, (near_x(-1), j, g))
-
     wait(GB.at[0], gsr)
 
     wait(EB.at[0], ebsr)
@@ -391,6 +376,21 @@
             send(TS, TB.at[slot], ts, tr, (near_x(d), far_y, 1 - g))
 
         send(TS, FB.at[slot], fs, fr, (near_x(d), j, g))
+
+    for m in range(6):
+        for t in range(2):
+            SY[m, t] = M2[2 + m, t, pl.ds(12, 8), :]
+
+    @pl.when(has_side)
+    def _():
+        send(SY, Y2.at[1 - g], ys.at[1], yr.at[1], (i, near_y(side), 1 - g))
+
+    send(SY, Y2.at[g], ys.at[0], yr.at[0], (i, j, 1 - g))
+    send(M2.at[pl.ds(4, 2), :, mid_rows, :], M2P.at[pl.ds(0, 2), :, mid_rows, :], xs, xr, (near_x(1), j, g))
+    send(M2.at[pl.ds(4, 2), :, mid_rows, :], M2P.at[pl.ds(8, 2), :, mid_rows, :], xs, xr, (near_x(-1), j, g))
+
+    send(V2.at[10, :, fine_rows, :], V2.at[2, :, fine_rows, :], vs, vr.at[0], (near_x(1), j, g))
+    send(V2.at[5, :, fine_rows, :], V2.at[13, :, fine_rows, :], vs, vr.at[1], (near_x(-1), j, g))
 
     wait(EB.at[pl.ds(0, 16)], ebr)
     lane = lanes_of(8)

time: 38.6 us -> 38.3 us (level)
  no operation moved by 1% of the time
where the time goes in v7:
time: 38.3 us; the launch traced here: 38.2 us
  Pallas kernels  35 us (91%)
  local copies, waits for them, and re-layouts  2.46 us (6%)
  between operations  0.67 us (2%)
    pallas_call x1, Pallas kernels, per_device(): pl.pallas_call(kernel, out_shape=jax.ShapeDtypeStruct(source.shape, F32),...  35 us
    unnamed x5, local copies, waits for them, and re-layouts  2.46 us

profile of v7, /device:TPU:25, one launch (start us, length us, event | category | flops | bytes accessed | tf_op | source)
XLA Modules:
  0.0 38.2 jit_solution(2450336660487259344)
XLA Ops:
  0.7 0.0 copy-start
  0.7 0.9 %copy-done = f32[8,32,128]{2,1,0:T(8,128)S(1)} copy-done((f32[8,32,128]{2,1,0:T(8,128)S(1)}, f32[8,32,128]{2,1,0:T(8,128)}, u32[]{:S(2)}) %copy-start) | copy-done | bytes 131096
  1.6 0.0 copy-start.1
  1.6 0.9 %copy-done.1 = f32[8,32,128]{2,1,0:T(8,128)S(1)} copy-done((f32[8,32,128]{2,1,0:T(8,128)S(1)}, f32[8,32,128]{2,1,0:T(8,128)}, u32[]{:S(2)}) %copy-start.1) | copy-done | bytes 131096
  2.5 35.0 %cycle.1 = f32[8,32,128]{2,1,0:T(8,128)S(1)} custom-call(f32[8,32,128]{2,1,0:T(8,128)S(1)} %copy-done, f32[8,32,128]{2,1,0:T(8,128)S(1)} %copy-done.1, s32[1,1,1]{2,1,0:T(1,128)S(6)} %copy.5.refs_2_), custom_call_target="tpu_custom_call" | custom-call | tf_op jit(solution)/shard_map/cycle/pallas_call | solution.py:611
  37.5 0.7 %copy.6 = f32[8,32,128]{2,1,0:T(8,128)} copy(f32[8,32,128]{2,1,0:T(8,128)S(1)} %cycle.1) | data formatting | bytes 262144
Async XLA Ops:
  0.7 0.9 %copy-start = (f32[8,32,128]{2,1,0:T(8,128)S(1)}, f32[8,32,128]{2,1,0:T(8,128)}, u32[]{:S(2)}) copy-start(f32[8,32,128]{2,1,0:T(8,128)} %refs_0_.1) | copy-start | bytes 393220
  1.6 0.9 %copy-start.1 = (f32[8,32,128]{2,1,0:T(8,128)S(1)}, f32[8,32,128]{2,1,0:T(8,128)}, u32[]{:S(2)}) copy-start(f32[8,32,128]{2,1,0:T(8,128)} %refs_1_.1) | copy-start | bytes 393220

commit v8 on v7

--- a/solution.py
+++ b/solution.py
@@ -389,9 +389,6 @@
     send(M2.at[pl.ds(4, 2), :, mid_rows, :], M2P.at[pl.ds(0, 2), :, mid_rows, :], xs, xr, (near_x(1), j, g))
     send(M2.at[pl.ds(4, 2), :, mid_rows, :], M2P.at[pl.ds(8, 2), :, mid_rows, :], xs, xr, (near_x(-1), j, g))
 
-    send(V2.at[10, :, fine_rows, :], V2.at[2, :, fine_rows, :], vs, vr.at[0], (near_x(1), j, g))
-    send(V2.at[5, :, fine_rows, :], V2.at[13, :, fine_rows, :], vs, vr.at[1], (near_x(-1), j, g))
-
     wait(EB.at[pl.ds(0, 16)], ebr)
     lane = lanes_of(8)
     row = lax.broadcasted_iota(jnp.int32, (8, 128), 0)
@@ -463,6 +460,9 @@
     @pl.when(has_side)
     def _():
         send(SQ, QP, qs, qr, (i, near_y(side), 1 - g))
+
+    send(V2.at[10, :, fine_rows, :], V2.at[2, :, fine_rows, :], vs, vr.at[0], (near_x(1), j, g))
+    send(V2.at[5, :, fine_rows, :], V2.at[13, :, fine_rows, :], vs, vr.at[1], (near_x(-1), j, g))
 
     for m in range(6):
         for t in range(2):

time: 38.3 us -> 38.3 us (level)
  no operation moved by 1% of the time
where the time goes in v8:
time: 38.3 us; the launch traced here: 38.2 us
  Pallas kernels  35 us (91%)
  local copies, waits for them, and re-layouts  2.46 us (6%)
  between operations  0.67 us (2%)
    pallas_call x1, Pallas kernels, per_device(): pl.pallas_call(kernel, out_shape=jax.ShapeDtypeStruct(source.shape, F32),...  35 us
    unnamed x5, local copies, waits for them, and re-layouts  2.46 us

profile of v8, /device:TPU:25, one launch (start us, length us, event | category | flops | bytes accessed | tf_op | source)
XLA Modules:
  0.0 38.2 jit_solution(14502545206126205292)
XLA Ops:
  0.7 0.0 copy-start
  0.7 0.9 %copy-done = f32[8,32,128]{2,1,0:T(8,128)S(1)} copy-done((f32[8,32,128]{2,1,0:T(8,128)S(1)}, f32[8,32,128]{2,1,0:T(8,128)}, u32[]{:S(2)}) %copy-start) | copy-done | bytes 131096
  1.6 0.0 copy-start.1
  1.6 0.9 %copy-done.1 = f32[8,32,128]{2,1,0:T(8,128)S(1)} copy-done((f32[8,32,128]{2,1,0:T(8,128)S(1)}, f32[8,32,128]{2,1,0:T(8,128)}, u32[]{:S(2)}) %copy-start.1) | copy-done | bytes 131096
  2.5 35.0 %cycle.1 = f32[8,32,128]{2,1,0:T(8,128)S(1)} custom-call(f32[8,32,128]{2,1,0:T(8,128)S(1)} %copy-done, f32[8,32,128]{2,1,0:T(8,128)S(1)} %copy-done.1, s32[1,1,1]{2,1,0:T(1,128)S(6)} %copy.5.refs_2_), custom_call_target="tpu_custom_call" | custom-call | tf_op jit(solution)/shard_map/cycle/pallas_call | solution.py:611
  37.5 0.7 %copy.6 = f32[8,32,128]{2,1,0:T(8,128)} copy(f32[8,32,128]{2,1,0:T(8,128)S(1)} %cycle.1) | data formatting | bytes 262144
Async XLA Ops:
  0.7 0.9 %copy-start = (f32[8,32,128]{2,1,0:T(8,128)S(1)}, f32[8,32,128]{2,1,0:T(8,128)}, u32[]{:S(2)}) copy-start(f32[8,32,128]{2,1,0:T(8,128)} %refs_0_.1) | copy-start | bytes 393220
  1.6 0.9 %copy-start.1 = (f32[8,32,128]{2,1,0:T(8,128)S(1)}, f32[8,32,128]{2,1,0:T(8,128)}, u32[]{:S(2)}) copy-start(f32[8,32,128]{2,1,0:T(8,128)} %refs_1_.1) | copy-start | bytes 393220
